TPU v7x, 32 devices: a whole 2x2x4 slice. The times are simulated.
32 devices in a mesh: groups: 2 (over x), brick: 8 (over z, y), chan: 2 (over core).
Axes of the slice: x: 2, y: 2, z: 4, core: 2. Of those that a mesh axis runs over, the one named last changes fastest.
Arguments:
- features: bfloat16 [32, 32768], P('chan', ('groups', 'brick')), parts along dimension 1, may hold values from -6 to 6
- pair_counts: int32 [16, 8], P(('groups', 'brick')), parts along dimension 0, may hold values from 1 to 2048, as said below
- pair_points: int32 [16, 8, 2048], P(('groups', 'brick')), parts along dimension 0, may hold values from 0 to 2047
- pair_cells: int32 [16, 8, 2048], P(('groups', 'brick')), parts along dimension 0, may hold values from 0 to 262143
- enc_weight: float32 [16, 8, 2048], P(('groups', 'brick')), parts along dimension 0, may hold values from 0.2 to 1
- dec_weight: float32 [16, 8, 2048], P(('groups', 'brick')), parts along dimension 0, may hold values from 0.1 to 1
- skip_weight: float32 [32, 32], P('chan'), may hold values from -1 to 1
- spectral_weight: float32 [2, 32, 32, 32, 1024], P(None, 'brick', None, None, 'chan'), may hold values from -2 to 2
- bias: float32 [32], P('chan'), may hold values from -3 to 3
Outputs:
- decoded: float32 [32, 32768], P('chan', ('groups', 'brick')), parts along dimension 1
There are 2 independent parts, one for each index of `groups`. A program takes and returns all parts, laid end to end along the dimension named above; an argument that names none is the same for every part. Nothing has to cross between parts.
Inputs may be any that keep to these rules, and one draw needn't show every extreme that they name: The first pair_counts[s, d] slots of brick s toward slab d hold pairs, the rest are padding. Every brick sends 1 or more pairs to every slab. In every draw one slab receives 2048 pairs from every brick.
All inputs are finite; a program needn't handle non-finite values.
Results may differ from a plain program's by a relative error of at most 0.0015.
Values may be sent and summed in bfloat16 or wider, within the bound.
A program may use at most 448 MiB of HBM per device.

v0:
```python
import math

import jax
import jax.numpy as jnp
from jax import lax
from jax.sharding import PartitionSpec as P

C = 32
G = 128
M = 32


def phase_table(length, freqs, signed):
    places = jnp.arange(length, dtype=jnp.int32)
    modes = jnp.arange(freqs, dtype=jnp.int32)
    if signed:
        modes = jnp.where(modes < freqs // 2, modes, modes - freqs + length)
    product = places[:, None] * modes[None, :] % length
    angle = product.astype(jnp.float32) * (2.0 * math.pi / length)
    return (jnp.cos(angle), jnp.sin(angle))


def shards(
    features,
    pair_counts,
    pair_points,
    pair_cells,
    enc_weight,
    dec_weight,
    skip_weight,
    spectral_weight,
    bias,
):
    highest = lax.Precision.HIGHEST
    bricks = lax.axis_size("brick")
    chans = features.shape[0]
    point_count = features.shape[1]
    slots = pair_points.shape[-1]
    planes = G // bricks
    slab_cells = planes * G * G
    valid = (jnp.arange(slots, dtype=jnp.int32)[None, :] < pair_counts[0][:, None]).astype(
        jnp.float32
    )
    enc_coef = (valid * enc_weight[0]).reshape(-1)
    dec_coef = (valid * dec_weight[0]).reshape(-1)
    point_index = pair_points[0].reshape(-1)
    cells_sent = pair_cells[0].astype(jnp.float32)[None]
    contrib = (features[:, point_index].astype(jnp.float32) * enc_coef[None, :]).reshape(
        chans, bricks, slots
    )
    got, got_cells = (
        lax.all_to_all(contrib, "brick", split_axis=1, concat_axis=1, tiled=True),
        lax.all_to_all(cells_sent, "brick", split_axis=1, concat_axis=1, tiled=True),
    )
    cells_in = got_cells[0].astype(jnp.int32).reshape(-1)
    latent = jnp.zeros((chans, slab_cells), jnp.float32).at[:, cells_in].add(got.reshape(chans, -1))
    skip = jnp.dot(
        skip_weight,
        lax.all_gather(latent, "chan", axis=0, tiled=True),
        precision=highest,
        preferred_element_type=jnp.float32,
    )
    scale = 1.0 / (G * math.sqrt(G))
    z_cos, z_sin = phase_table(G, M, False)
    y_cos, y_sin = phase_table(G, M, True)
    x_cos, x_sin = phase_table(G, M, True)
    field = latent.reshape(chans, planes, G, G)
    z_real = jnp.einsum("cxyz,zk->cxyk", field, z_cos, precision=highest)
    z_imag = -jnp.einsum("cxyz,zk->cxyk", field, z_sin, precision=highest)
    y_real = jnp.einsum("cxyk,yb->cxbk", z_real, y_cos, precision=highest) + jnp.einsum(
        "cxyk,yb->cxbk", z_imag, y_sin, precision=highest
    )
    y_imag = jnp.einsum("cxyk,yb->cxbk", z_imag, y_cos, precision=highest) - jnp.einsum(
        "cxyk,yb->cxbk", z_real, y_sin, precision=highest
    )
    partial_spec = jnp.stack([y_real, y_imag])
    pencil = lax.all_to_all(
        lax.all_to_all(partial_spec, "brick", split_axis=3, concat_axis=2, tiled=True),
        "chan",
        split_axis=4,
        concat_axis=1,
        tiled=True,
    )
    p_real = pencil[0]
    p_imag = pencil[1]
    c_real = jnp.einsum("cxbk,xa->bcka", p_real, x_cos, precision=highest) + jnp.einsum(
        "cxbk,xa->bcka", p_imag, x_sin, precision=highest
    )
    c_imag = jnp.einsum("cxbk,xa->bcka", p_imag, x_cos, precision=highest) - jnp.einsum(
        "cxbk,xa->bcka", p_real, x_sin, precision=highest
    )
    y_local = c_real.shape[0]
    z_local = c_real.shape[2]
    c_real = (c_real * scale).reshape(y_local, C, z_local * M)
    c_imag = (c_imag * scale).reshape(y_local, C, z_local * M)
    w_real = spectral_weight[0]
    w_imag = spectral_weight[1]
    m_real = jnp.einsum("bioq,biq->boq", w_real, c_real, precision=highest) - jnp.einsum(
        "bioq,biq->boq", w_imag, c_imag, precision=highest
    )
    m_imag = jnp.einsum("bioq,biq->boq", w_real, c_imag, precision=highest) + jnp.einsum(
        "bioq,biq->boq", w_imag, c_real, precision=highest
    )
    m_real = m_real.reshape(y_local, C, z_local, M)
    m_imag = m_imag.reshape(y_local, C, z_local, M)
    i_real = jnp.einsum("boka,xa->oxbk", m_real, x_cos, precision=highest) - jnp.einsum(
        "boka,xa->oxbk", m_imag, x_sin, precision=highest
    )
    i_imag = jnp.einsum("boka,xa->oxbk", m_real, x_sin, precision=highest) + jnp.einsum(
        "boka,xa->oxbk", m_imag, x_cos, precision=highest
    )
    mixed_x = jnp.stack([i_real, i_imag])
    returned = lax.all_to_all(
        lax.all_to_all(mixed_x, "brick", split_axis=2, concat_axis=3, tiled=True),
        "chan",
        split_axis=1,
        concat_axis=4,
        tiled=True,
    )
    r_real = returned[0]
    r_imag = returned[1]
    v_real = jnp.einsum("cxbk,yb->cxyk", r_real, y_cos, precision=highest) - jnp.einsum(
        "cxbk,yb->cxyk", r_imag, y_sin, precision=highest
    )
    v_imag = jnp.einsum("cxbk,yb->cxyk", r_real, y_sin, precision=highest) + jnp.einsum(
        "cxbk,yb->cxyk", r_imag, y_cos, precision=highest
    )
    factor = jnp.where(jnp.arange(M) == 0, 1.0, 2.0).astype(jnp.float32)
    spectral = jnp.einsum(
        "cxyk,zk->cxyz", v_real, z_cos * factor[None, :], precision=highest
    ) - jnp.einsum("cxyk,zk->cxyz", v_imag, z_sin * factor[None, :], precision=highest)
    spectral = spectral.reshape(chans, slab_cells) * scale
    hidden = jax.nn.gelu(spectral + skip + bias[:, None], approximate=True).astype(jnp.bfloat16)
    requested = hidden[:, cells_in].reshape(chans, bricks, slots)
    answered = lax.all_to_all(requested, "brick", split_axis=1, concat_axis=1, tiled=True)
    rows = answered.reshape(chans, -1).astype(jnp.float32) * dec_coef[None, :]
    decoded = jnp.zeros((chans, point_count), jnp.float32).at[:, point_index].add(rows)
    return decoded


def solution(mesh):
    return jax.shard_map(
        shards,
        mesh=mesh,
        in_specs=(
            P("chan", ("groups", "brick")),
            P(("groups", "brick"), None),
            P(("groups", "brick"), None, None),
            P(("groups", "brick"), None, None),
            P(("groups", "brick"), None, None),
            P(("groups", "brick"), None, None),
            P("chan", None),
            P(None, "brick", None, None, "chan"),
            P("chan"),
        ),
        out_specs=P("chan", ("groups", "brick")),
        check_vma=False,
    )
```

profile of v0, /device:TPU:0, one launch (start us, length us, event | category | flops | bytes accessed | tf_op | source)
XLA Modules:
  0.0 1777.3 jit_solution(6401762983431265013)
XLA Ops:
  8.1 7.3 all-to-all-start
  18.1 57.4 %gather_fusion = bf16[16384,16]{1,0:T(8,128)(2,1)} fusion(bf16[16,2048]{0,1:T(8,128)(2,1)S(1)} %copy.152, s32[16384]{0:T(1024)S(1)} %broadcast_clamp_fusion.2), kind=kCustom, calls=%fused_computation | custom fusion | bytes 1114112 | tf_op jit(solution)/shard_map/gather | solution.py:48
  75.5 5.1 convert_element_type.90
  80.6 5.1 copy.153
  86.9 6.0 all-to-all-start.1
  93.1 7.1 sort
  100.3 18.0 %all-to-all-done.1 = f32[16,8,2048]{2,0,1:T(8,128)S(1)} async-done(((f32[16,8,2048]{2,0,1:T(8,128)}), f32[16,8,2048]{2,0,1:T(8,128)S(1)}, u32[]{:S(2)}, u32[]{:S(2)}) %all-to-all-start.1) | async-done | bytes 1048608 | tf_op jit(solution)/shard_map/all_to_all | solution.py:52
  118.4 5.0 copy.155
  123.4 237.5 %scatter_custom_fusion = f32[16,262144]{0,1:T(8,128)} fusion(s32[16384]{0:T(1024)S(1)} %get-tuple-element.5, f32[]{:T(128)} %constant.20.clone.1, f32[16384,16]{1,0:T(8,128)} %copy.155, s32[16384]{0:T(1024)S(1)} %broadcast_clamp_fusion.1), kind=kCustom, calls=%fused_computation.8 | custom fusion | flops 262144 | bytes 16777728 | tf_op jit(solution)/shard_map/scatter-add | solution.py:56
  360.9 70.2 %copy.178 = f32[16,262144]{1,0:T(8,128)} copy(f32[16,262144]{0,1:T(8,128)} %scatter_custom_fusion) | data formatting | bytes 33554432 | tf_op jit(solution)/shard_map/scatter-add | solution.py:56
  431.2 233.9 %fusion.56 = f32[16,16,128,32]{3,0,2,1:T(8,128)} fusion(f32[16,16,128,128]{0,3,2,1:T(8,128)} %bitcast.19), kind=kOutput, calls=%fused_computation.88 | convolution fusion | flops 1610670080 | bytes 20971520 | tf_op jit(solution)/shard_map/cxyz,zk->cxyk/dot_general | solution.py:68
  665.1 11.4 copy.157
  676.5 216.4 %fusion.54 = f32[16,16,128,32]{3,0,2,1:T(8,128)} fusion(f32[16,16,128,128]{0,3,2,1:T(8,128)} %bitcast.19), kind=kOutput, calls=%fused_computation.86 | convolution fusion | flops 1610670080 | bytes 20971520 | tf_op jit(solution)/shard_map/cxyz,zk->cxyk/dot_general | solution.py:69
  892.9 11.4 copy.159
  904.3 21.3 %fusion.80 = f32[32,16,16,32]{3,0,2,1:T(8,128)S(1)} fusion(f32[16,16,128,32]{2,3,1,0:T(8,128)} %copy.157, s32[32]{0:T(128)S(1)} %compare_select_fusion.2), kind=kOutput, calls=%fused_computation.112 | convolution fusion | flops 402710528 | bytes 5243008 | tf_op jit(solution)/shard_map/cxyk,yb->cxbk/dot_general | solution.py:70
  925.6 19.7 %add_bitcast_fusion = f32[1,16,16,32,32]{4,3,2,1,0:T(8,128)S(1)} fusion(f32[32,16,16,32]{3,0,2,1:T(8,128)S(1)} %fusion.80, f32[16,16,128,32]{2,3,1,0:T(8,128)S(1)} %copy-done.2, s32[32]{0:T(128)S(1)} %compare_select_fusion.2), kind=kOutput, calls=%fused_computation.36 | convolution fusion | flops 404021248 | bytes 6291584 | tf_op jit(solution)/shard_map/cxyk,yb->cxbk/dot_general | solution.py:70
  945.4 19.4 %fusion.66 = f32[32,16,16,32]{3,0,2,1:T(8,128)S(1)} fusion(f32[16,16,128,32]{2,3,1,0:T(8,128)S(1)} %copy-done.1, s32[32]{0:T(128)S(1)} %compare_select_fusion.2), kind=kOutput, calls=%fused_computation.98 | convolution fusion | flops 402710528 | bytes 5243008 | tf_op jit(solution)/shard_map/cxyk,yb->cxbk/dot_general | solution.py:73
  964.8 19.6 %subtract_bitcast_fusion = f32[1,16,16,32,32]{4,3,2,1,0:T(8,128)S(1)} fusion(f32[32,16,16,32]{3,0,2,1:T(8,128)S(1)} %fusion.66, f32[16,16,128,32]{2,3,1,0:T(8,128)S(1)} %copy-done.2, s32[32]{0:T(128)S(1)} %compare_select_fusion.2), kind=kOutput, calls=%fused_computation.35 | convolution fusion | flops 404021248 | bytes 6291584 | tf_op jit(solution)/shard_map/cxyk,yb->cxbk/dot_general | solution.py:73
  986.0 8.1 copy.241
  994.1 7.4 reshape.200
  1001.6 52.7 %all_to_all.81 = f32[8,1,65536]{2,1,0:T(1,128)} all-to-all(f32[8,1,65536]{2,1,0:T(1,128)S(1)} %reshape.200), channel_id=1, replica_groups=mesh['groups'=2,'brick'=8,'chan'=2] {'brick'}, dimensions={0} | all-to-all | bytes 4194304 | tf_op jit(solution)/shard_map/all_to_all | solution.py:78
  1054.8 7.4 reduce.8
  1062.2 6.0 reshape.201
  1068.1 7.9 copy.162
  1076.0 5.5 copy.163
  1081.6 5.4 all_to_all.82
  1089.7 4.9 fusion.75
  1099.8 4.9 fusion.77
  1104.8 5.3 fusion.36
  1110.4 8.1 fusion.17
  1124.5 7.5 copy.171
  1132.0 8.6 reshape.202
  1145.3 48.8 %all-to-all-done.4 = f32[8,1,65536]{2,1,0:T(1,128)} async-done(((f32[8,1,65536]{2,1,0:T(1,128)}), f32[8,1,65536]{2,1,0:T(1,128)}, u32[]{:S(2)}, u32[]{:S(2)}) %all-to-all-start.4) | async-done | bytes 2097184 | tf_op jit(solution)/shard_map/all_to_all | solution.py:114
  1194.0 7.4 reduce.9
  1201.4 5.9 reshape.203
  1207.4 8.3 copy.173
  1215.6 11.3 copy.174
  1227.0 5.9 reshape.204
  1232.8 6.3 all_to_all.83
  1239.2 8.8 reduce.10
  1247.9 6.4 reshape.205
  1276.6 27.2 %fusion.21 = f32[16,16,128,128]{3,2,1,0:T(8,128)S(1)} fusion(f32[128,16,16,32]{0,3,2,1:T(8,128)S(1)} %fusion.71, f32[128,16,16,32]{0,3,2,1:T(8,128)S(1)} %fusion.60, f32[32]{0:T(128)S(1)} %compare_select_fusion.3), kind=kOutput, calls=%fused_computation.31 | convolution fusion | flops 1611722752 | bytes 25165952 | tf_op jit(solution)/shard_map/cxyk,zk->cxyz/dot_general | solution.py:129
  1303.8 29.2 %subtract_multiply_fusion = f32[16,16,128,128]{3,2,1,0:T(8,128)} fusion(f32[16,16,128,128]{3,2,1,0:T(8,128)S(1)} %fusion.21, f32[128,16,16,32]{0,3,2,1:T(8,128)S(1)} %fusion.58, f32[128,16,16,32]{0,3,2,1:T(8,128)S(1)} %fusion.69, f32[32]{0:T(128)S(1)} %compare_select_fusion.3), kind=kOutput, calls=%fused_computation.19 | convolution fusion | flops 1620111360 | bytes 41943168 | tf_op jit(solution)/shard_map/cxyk,zk->cxyz/dot_general | solution.py:131
  1333.0 32.5 %fusion.12 = bf16[16,262144]{1,0:T(8,128)(2,1)} fusion(f32[32,262144]{1,0:T(8,128)} %all-gather.2.cloned.1.call-done, f32[16,32]{1,0:T(8,128)S(1)} %copy-done, f32[2,8,2048,128]{3,2,1,0:T(8,128)} %bitcast.210, f32[16]{0:T(128)S(1)} %copy-done.8), kind=kOutput, calls=%fused_computation.18 | convolution fusion | flops 1656750080 | bytes 58722368 | tf_op jit(solution)/shard_map/dot_general | solution.py:57
  1365.5 44.6 %copy.179 = bf16[16,262144]{0,1:T(8,128)(2,1)} copy(bf16[16,262144]{1,0:T(8,128)(2,1)} %fusion.12) | data formatting | bytes 16777216 | tf_op jit(solution)/shard_map/convert_element_type | solution.py:133
  1410.1 243.4 %gather_fusion.1 = bf16[16384,16]{1,0:T(8,128)(2,1)} fusion(bf16[16,262144]{0,1:T(8,128)(2,1)} %copy.179, s32[16384]{0:T(1024)S(1)} %broadcast_clamp_fusion), kind=kCustom, calls=%fused_computation.1 | custom fusion | bytes 1114112 | tf_op jit(solution)/shard_map/gather | solution.py:134
  1661.9 14.6 all-to-all-done.6
  1681.4 87.8 %scatter_custom_fusion.1 = f32[16,2048]{0,1:T(8,128)S(1)} fusion(s32[16384]{0:T(1024)} %bitcast.239, f32[16384,16]{1,0:T(8,128)} %copy.182, f32[]{:T(128)} %constant.20.clone.1), kind=kCustom, calls=%fused_computation.59 | custom fusion | flops 262144 | bytes 131584 | tf_op jit(solution)/shard_map/scatter-add | solution.py:137
  (79 shorter events, 63.1 us)
Async XLA Ops:
  6.5 1326.5 %copy-start = (f32[16,32]{1,0:T(8,128)S(1)}, f32[16,32]{1,0:T(8,128)}, u32[]{:S(2)}) copy-start(f32[16,32]{1,0:T(8,128)} %param.15) | copy-start | bytes 6148
  8.1 78.8 %all-to-all-start = ((f32[1,8,2048]{2,0,1:T(1,128)}), f32[1,8,2048]{2,0,1:T(1,128)S(1)}, u32[]{:S(2)}, u32[]{:S(2)}) async-start(f32[1,8,2048]{2,0,1:T(1,128)} %copy.151), calls=%async_computation | async-start | bytes 131072 | tf_op jit(solution)/shard_map/all_to_all | solution.py:53
  16.4 0.6 copy-start.5
  80.6 5.1 copy-start.6
  80.6 5.2 copy-start.9
  86.9 31.4 %all-to-all-start.1 = ((f32[16,8,2048]{2,0,1:T(8,128)}), f32[16,8,2048]{2,0,1:T(8,128)S(1)}, u32[]{:S(2)}, u32[]{:S(2)}) async-start(f32[16,8,2048]{2,0,1:T(8,128)} %broadcast_multiply_fusion), calls=%async_computation.1 | async-start | bytes 2097152 | tf_op jit(solution)/shard_map/all_to_all | solution.py:52
  92.9 1240.1 %all-gather.2.cloned.1.call-start = ((), (), s32[]{:S(2)}) async-start(), calls=%async_computation.7 | async-start | bytes 50331648 | tf_op jit(solution)/shard_map/all_gather | solution.py:59
  93.1 25.3 %copy-start.3 = (s32[16384,1]{0,1:T(1,128)}, s32[16384,1]{0,1:T(1,128)S(1)}, u32[]{:S(2)}) copy-start(s32[16384,1]{0,1:T(1,128)S(1)} %compare_select_fusion) | copy-start | bytes 196612
  904.3 21.3 %copy-start.2 = (f32[16,16,128,32]{2,3,1,0:T(8,128)S(1)}, f32[16,16,128,32]{2,3,1,0:T(8,128)}, u32[]{:S(2)}) copy-start(f32[16,16,128,32]{2,3,1,0:T(8,128)} %copy.159) | copy-start | bytes 12582916
  925.6 19.7 %copy-start.1 = (f32[16,16,128,32]{2,3,1,0:T(8,128)S(1)}, f32[16,16,128,32]{2,3,1,0:T(8,128)}, u32[]{:S(2)}) copy-start(f32[16,16,128,32]{2,3,1,0:T(8,128)} %copy.157) | copy-start | bytes 12582916
  1140.6 4.7 copy-start.4
  1140.6 53.5 %all-to-all-start.4 = ((f32[8,1,65536]{2,1,0:T(1,128)}), f32[8,1,65536]{2,1,0:T(1,128)}, u32[]{:S(2)}, u32[]{:S(2)}) async-start(f32[8,1,65536]{2,1,0:T(1,128)} %reshape.202), calls=%async_computation.4 | async-start | bytes 4194304 | tf_op jit(solution)/shard_map/all_to_all | solution.py:114
  1303.8 29.3 %copy-start.8 = (f32[16]{0:T(128)S(1)}, f32[16]{0:T(128)}, u32[]{:S(2)}) copy-start(f32[16]{0:T(128)} %param.17) | copy-start | bytes 196
  1410.1 251.6 %copy-start.10 = (s32[1,8]{1,0:T(1,128)S(1)}, s32[1,8]{1,0:T(1,128)}, u32[]{:S(2)}) copy-start(s32[1,8]{1,0:T(1,128)} %param.10) | copy-start | bytes 100
  1410.1 251.7 %copy-start.7 = (f32[1,8,2048]{2,1,0:T(8,128)S(1)}, f32[1,8,2048]{2,1,0:T(8,128)}, u32[]{:S(2)}) copy-start(f32[1,8,2048]{2,1,0:T(8,128)} %param.14) | copy-start | bytes 196612
  1658.0 18.6 %all-to-all-start.6 = ((bf16[16,8,2048]{2,0,1:T(8,128)(2,1)}), bf16[16,8,2048]{2,0,1:T(8,128)(2,1)S(1)}, u32[]{:S(2)}, u32[]{:S(2)}) async-start(bf16[16,8,2048]{2,0,1:T(8,128)(2,1)} %copy.180), calls=%async_computation.6 | async-start | bytes 1048576 | tf_op jit(solution)/shard_map/all_to_all | solution.py:135
Sparse Core Ops, SparseCore 0:
  431.3 49.9 all-gather.1
where the time goes:
time: 1780 us
  matrix products  661 us (37%)
  local copies, waits for them, and re-layouts  561 us (32%)
  other arithmetic  374 us (21%)
  waiting for transfers between devices  81.5 us (5%)
  blocking collectives  64.4 us (4%)
  starting transfers between devices  21.7 us (1%)
    scatter-add x3, other arithmetic, shards(): jnp.zeros((chans, slab_cells), jnp.float32).at[:, cells_in]  245 us
    gather x1, local copies, waits for them, and re-layouts, shards(): requested = hidden[:, cells_in].reshape(chans, bricks, slots)  243 us
    dot_general x1, matrix products, shards(): z_real = jnp.einsum('cxyz,zk->cxyk', field, z_cos, precision=highest)  234 us
    dot_general x1, matrix products, shards(): z_imag = -jnp.einsum('cxyz,zk->cxyk', field, z_sin, precision=highest)  216 us
    scatter-add x1, other arithmetic, shards(): jnp.zeros((chans, point_count), jnp.float32).at[:, point_index].add(rows)  87.8 us
    scatter-add x2, local copies, waits for them, and re-layouts, shards(): jnp.zeros((chans, slab_cells), jnp.float32).at[:, cells_in]  70.2 us
    gather x1, local copies, waits for them, and re-layouts, shards(): features[:, point_index].astype(jnp.float32) * enc_coef[None, :]  57.4 us
    all_to_all x1, blocking collectives, shards(): lax.all_to_all(partial_spec, 'brick', split_axis=3, concat_axis=2, tiled=...  52.7 us
  transfers between devices with their start and end apart: 5, of which 3 were waited for; matrix products, arithmetic and copies ran while one was open for 48% of the time, Pallas kernels for 0%

commit v1 on v0

v1 whole, which is shorter than its diff:
```python
import math

import jax
import jax.numpy as jnp
import numpy as np
from jax import lax
from jax.experimental import pallas as pl
from jax.experimental.pallas import tpu as pltpu
from jax.sharding import PartitionSpec as P

C = 32
G = 128
M = 32
F32 = jnp.float32
BF16 = jnp.bfloat16
NT = (((1,), (1,)), ((), ()))


def angles(freqs, signed):
    places = np.arange(G)
    modes = np.arange(freqs)
    if signed:
        modes = np.where(modes < freqs // 2, modes, modes - freqs + G)
    angle = (modes[:, None] * places[None, :] % G) * (2.0 * math.pi / G)
    return np.cos(angle), np.sin(angle)


def params(mib=48):
    return pltpu.CompilerParams(
        dimension_semantics=("arbitrary",), vmem_limit_bytes=mib * 1024 * 1024
    )


def mm(a, b):
    return jnp.dot(a, b, preferred_element_type=F32)


def hot(index, rows):
    places = lax.broadcasted_iota(jnp.int32, (rows, index.shape[1]), 0)
    return jnp.where(places == index, 1.0, 0.0).astype(BF16)


def pick_kernel(chans, high, table_ref, points_ref, out_ref):
    points = points_ref[...]
    rows = mm(table_ref[...], hot(points & 127, 128)).reshape(chans, high, points.shape[1])
    keep = lax.broadcasted_iota(jnp.int32, (1, high, points.shape[1]), 1) == (points >> 7)[None]
    out_ref[...] = jnp.sum(jnp.where(keep, rows, 0.0), axis=1).astype(BF16)


def pick(features, points, step=1024):
    chans, count = features.shape
    high = count // 128
    total = points.shape[1]
    return pl.pallas_call(
        lambda *r: pick_kernel(chans, high, *r),
        grid=(total // step,),
        in_specs=[
            pl.BlockSpec((chans * high, 128), lambda i: (0, 0)),
            pl.BlockSpec((1, step), lambda i: (0, i)),
        ],
        out_specs=pl.BlockSpec((chans, step), lambda i: (0, i)),
        out_shape=jax.ShapeDtypeStruct((chans, total), BF16),
        compiler_params=params(),
    )(features.reshape(chans * high, 128), points)


def y_phases(tab_ref, y):
    both = mm(tab_ref[...], hot(y, G))
    return both[: 2 * M] + both[2 * M :]


def forward_kernel(chans, width, wins, span_ref, feat_ref, coef_ref, cell_ref, ytab_ref, ztab_ref, out_ref, acc_ref):
    step = pl.program_id(0)

    @pl.when(step == 0)
    def _():
        acc_ref[...] = jnp.zeros_like(acc_ref)

    first, last = span_ref[0, step], span_ref[1, step]
    planes = width * wins

    @pl.when(first < planes)
    def _():
        cells = cell_ref[...]
        x = cells >> 14
        count = cells.shape[1]
        ys = y_phases(ytab_ref, (cells >> 7) & 127)
        zs = mm(ztab_ref[...], hot(cells & 127, G))
        feats = feat_ref[...].astype(F32) * coef_ref[...]
        left = (feats[:, None, :] * ys[None]).astype(BF16).reshape(chans * 2 * M, count)
        for win in range(wins):
            @pl.when((first < (win + 1) * width) & (last >= win * width))
            def _():
                pieces = []
                for part in range(4):
                    piece = zs[part * 16 : part * 16 + 16]
                    for off in range(width):
                        pieces.append(jnp.where(x == win * width + off, piece, 0.0))
                right = jnp.concatenate(pieces, axis=0).astype(BF16)
                acc_ref[win] += lax.dot_general(left, right, NT, preferred_element_type=F32)

    @pl.when(step == pl.num_programs(0) - 1)
    def _():
        half = 2 * width * 16
        for win in range(wins):
            full = acc_ref[win].reshape(chans, 2 * M, 2 * half)
            out_ref[0, win] = (full[:, :M, :half] - full[:, M:, half:]).astype(BF16)
            out_ref[1, win] = (-full[:, :M, half:] - full[:, M:, :half]).astype(BF16)


def forward(feats, coef, cells, span, planes, step):
    chans, total = feats.shape
    width = min(8, planes)
    wins = planes // width
    y_cos, y_sin = angles(M, True)
    z_cos, z_sin = angles(M, False)
    ytab = np.concatenate([y_cos, y_sin]).astype(np.float32)
    yhi = ytab.astype(BF16)
    ylo = (ytab - yhi.astype(np.float32)).astype(BF16)
    ytab = jnp.asarray(np.concatenate([yhi, ylo]))
    ztab = jnp.asarray(np.concatenate([z_cos, z_sin]).astype(BF16))
    lanes = 2 * width * 16
    return pl.pallas_call(
        lambda *r: forward_kernel(chans, width, wins, *r),
        grid_spec=pltpu.PrefetchScalarGridSpec(
            num_scalar_prefetch=1,
            grid=(total // step,),
            in_specs=[
                pl.BlockSpec((chans, step), lambda i, s: (0, i)),
                pl.BlockSpec((1, step), lambda i, s: (0, i)),
                pl.BlockSpec((1, step), lambda i, s: (0, i)),
                pl.BlockSpec((4 * M, G), lambda i, s: (0, 0)),
                pl.BlockSpec((2 * M, G), lambda i, s: (0, 0)),
            ],
            out_specs=pl.BlockSpec((2, wins, chans, M, lanes), lambda i, s: (0, 0, 0, 0, 0)),
            scratch_shapes=[pltpu.VMEM((wins, chans * 2 * M, 2 * lanes), F32)],
        ),
        out_shape=jax.ShapeDtypeStruct((2, wins, chans, M, lanes), BF16),
        compiler_params=params(),
    )(span, feats, coef, cells, ytab, ztab)


def skip_kernel(lists, per, wide, bounds_ref, rounds_ref, mine_ref, cells_ref, vals_ref, w_ref, out_ref):
    step = pl.program_id(0)
    mine = mine_ref[...]
    lanes = 128

    def one(turn, acc):
        hits = []
        vals = []
        for src in range(lists):
            for off in range(wide):
                at = bounds_ref[step, 2 * src] + turn * wide + off
                live = at < bounds_ref[step, 2 * src + 1]
                row = src * per + jnp.where(live, at, 0)
                other = jnp.where(live, cells_ref[pl.ds(row, 1), :], -1)
                hits.append(jnp.where(mine == other, 1.0, 0.0).astype(BF16))
                vals.append(vals_ref[row])
        hit = jnp.concatenate(hits, axis=1)
        val = jnp.concatenate(vals, axis=1)
        return acc + lax.dot_general(val, hit, NT, preferred_element_type=F32)

    acc = lax.fori_loop(0, rounds_ref[step], one, jnp.zeros((2 * C, lanes), F32))
    latent = acc[:C] + acc[C:]
    out_ref[...] = jnp.dot(
        w_ref[...], latent, precision=lax.Precision.HIGHEST, preferred_element_type=F32
    )


def skip_at(feats, coef, cells, weight, lists, slots, slab_cells, wide=2):
    total = cells.shape[1]
    per = slots // 128
    chunks = total // 128
    vals = feats.astype(F32) * coef
    hi = lax.reduce_precision(vals, 8, 7)
    lo = (vals - hi).astype(BF16)
    both = jnp.concatenate([hi.astype(BF16), lo], axis=0)
    both = both.reshape(2 * C, chunks, 128).transpose(1, 0, 2)
    rows = cells.reshape(chunks, 128)
    low = rows[:, 0]
    high = jnp.minimum(rows[:, 127], slab_cells - 1)
    q_low = low.reshape(1, lists, per)
    q_high = rows[:, 127].reshape(1, lists, per)
    start = jnp.sum((q_high < low[:, None, None]).astype(jnp.int32), axis=2)
    end = jnp.sum((q_low <= high[:, None, None]).astype(jnp.int32), axis=2)
    end = jnp.where(low[:, None] >= slab_cells, start, jnp.maximum(end, start))
    rounds = jnp.max((end - start + wide - 1) // wide, axis=1)
    bounds = jnp.stack([start, end], axis=2).reshape(chunks, 2 * lists)
    return pl.pallas_call(
        lambda *r: skip_kernel(lists, per, wide, *r),
        grid_spec=pltpu.PrefetchScalarGridSpec(
            num_scalar_prefetch=2,
            grid=(chunks,),
            in_specs=[
                pl.BlockSpec((128, 1), lambda i, a, b: (i, 0)),
                pl.BlockSpec((chunks, 128), lambda i, a, b: (0, 0)),
                pl.BlockSpec((chunks, 2 * C, 128), lambda i, a, b: (0, 0, 0)),
                pl.BlockSpec(weight.shape, lambda i, a, b: (0, 0)),
            ],
            out_specs=pl.BlockSpec((weight.shape[0], 128), lambda i, a, b: (0, i)),
        ),
        out_shape=jax.ShapeDtypeStruct((weight.shape[0], total), F32),
        compiler_params=params(),
    )(bounds, rounds, cells.reshape(total, 1), rows, both, weight)


def inverse_kernel(chans, width, wins, span_ref, cell_ref, skip_ref, bias_ref, r_ref, ytab_ref, ztab_ref, out_ref, acc_ref):
    step = pl.program_id(0)
    first, last = span_ref[0, step], span_ref[1, step]
    planes = width * wins

    @pl.when(first >= planes)
    def _():
        out_ref[...] = jnp.zeros_like(out_ref)

    @pl.when(first < planes)
    def _():
        cells = cell_ref[...]
        count = cells.shape[1]
        x = cells >> 14
        acc_ref[...] = jnp.zeros_like(acc_ref)
        zs = mm(ztab_ref[...], hot(cells & 127, G))
        for win in range(wins):
            @pl.when((first < (win + 1) * width) & (last >= win * width))
            def _():
                pieces = [jnp.where(x == win * width + off, zs, 0.0) for off in range(width)]
                right = jnp.concatenate(pieces, axis=0).astype(BF16)
                acc_ref[...] += mm(r_ref[win], right)
        ys = y_phases(ytab_ref, (cells >> 7) & 127)
        field = jnp.sum(acc_ref[...].reshape(chans, 2 * M, count) * ys[None], axis=1)
        v = field * (1.0 / (G * math.sqrt(G))) + skip_ref[...] + bias_ref[...]
        out_ref[...] = jax.nn.gelu(v, approximate=True).astype(BF16)


def inverse(cells, skip, bias, mat, span, planes, step):
    chans, total = skip.shape
    width = min(4, planes)
    wins = planes // width
    y_cos, y_sin = angles(M, True)
    z_cos, z_sin = angles(M, False)
    ytab = np.concatenate([y_cos, y_sin]).astype(np.float32)
    yhi = ytab.astype(BF16)
    ylo = (ytab - yhi.astype(np.float32)).astype(BF16)
    ytab = jnp.asarray(np.concatenate([yhi, ylo]))
    factor = np.where(np.arange(M) == 0, 1.0, 2.0)[:, None]
    ztab = jnp.asarray(np.concatenate([z_cos * factor, z_sin * factor]).astype(BF16))
    return pl.pallas_call(
        lambda *r: inverse_kernel(chans, width, wins, *r),
        grid_spec=pltpu.PrefetchScalarGridSpec(
            num_scalar_prefetch=1,
            grid=(total // step,),
            in_specs=[
                pl.BlockSpec((1, step), lambda i, s: (0, i)),
                pl.BlockSpec((chans, step), lambda i, s: (0, i)),
                pl.BlockSpec((chans, 1), lambda i, s: (0, 0)),
                pl.BlockSpec(mat.shape, lambda i, s: (0, 0, 0)),
                pl.BlockSpec((4 * M, G), lambda i, s: (0, 0)),
                pl.BlockSpec((2 * M, G), lambda i, s: (0, 0)),
            ],
            out_specs=pl.BlockSpec((chans, step), lambda i, s: (0, i)),
            scratch_shapes=[pltpu.VMEM((chans * 2 * M, step), F32)],
        ),
        out_shape=jax.ShapeDtypeStruct((chans, total), BF16),
        compiler_params=params(),
    )(span, cells, skip, bias[:, None], mat, ytab, ztab)


def decode_kernel(chans, high, hid_ref, coef_ref, points_ref, out_ref):
    @pl.when(pl.program_id(0) == 0)
    def _():
        out_ref[...] = jnp.zeros_like(out_ref)

    points = points_ref[...]
    count = points.shape[1]
    vals = hid_ref[...].astype(F32) * coef_ref[...]
    hi = vals.astype(BF16).astype(F32)
    lo = vals - hi
    keep = lax.broadcasted_iota(jnp.int32, (1, high, count), 1) == (points >> 7)[None]
    low_hot = hot(points & 127, 128)
    total = jnp.zeros((chans * high, 128), F32)
    for part in (hi, lo):
        spread = jnp.where(keep, part[:, None, :], 0.0).astype(BF16).reshape(chans * high, count)
        total += lax.dot_general(spread, low_hot, NT, preferred_element_type=F32)
    out_ref[...] += total


def decode(hidden, coef, points, count, step=1024):
    chans, total = hidden.shape
    high = count // 128
    out = pl.pallas_call(
        lambda *r: decode_kernel(chans, high, *r),
        grid=(total // step,),
        in_specs=[
            pl.BlockSpec((chans, step), lambda i: (0, i)),
            pl.BlockSpec((1, step), lambda i: (0, i)),
            pl.BlockSpec((1, step), lambda i: (0, i)),
        ],
        out_specs=pl.BlockSpec((chans * high, 128), lambda i: (0, 0)),
        out_shape=jax.ShapeDtypeStruct((chans * high, 128), F32),
        compiler_params=params(),
    )(hidden, coef, points)
    return out.reshape(chans, count)


def shards(
    features,
    pair_counts,
    pair_points,
    pair_cells,
    enc_weight,
    dec_weight,
    skip_weight,
    spectral_weight,
    bias,
):
    bricks = lax.axis_size("brick")
    pair = lax.axis_size("chan")
    chans, point_count = features.shape
    slots = pair_points.shape[-1]
    planes = G // bricks
    slab_cells = planes * G * G
    step = 256
    both = ("brick", "chan")

    valid = jnp.arange(slots, dtype=jnp.int32)[None, :] < pair_counts[0][:, None]
    key = jnp.where(valid, pair_cells[0], slab_cells)
    enc = jnp.where(valid, enc_weight[0], 0.0)
    dec = jnp.where(valid, dec_weight[0], 0.0)
    key, points, enc, dec = lax.sort(
        (key, pair_points[0], enc, dec), dimension=1, num_keys=1, is_stable=False
    )
    points = points.reshape(1, -1)
    picked = pick(features, points)

    meta = jnp.stack([key.astype(F32), enc], axis=1)
    meta = lax.all_to_all(meta, "brick", split_axis=0, concat_axis=0, tiled=True)
    cells = meta[:, 0].astype(jnp.int32).reshape(1, -1)
    coef = meta[:, 1].reshape(1, -1)
    got = lax.all_to_all(
        picked.reshape(chans, bricks, slots), "brick", split_axis=1, concat_axis=1, tiled=True
    ).reshape(chans, -1)
    every = lax.all_gather(got, "chan", axis=0, tiled=True)

    by_step = cells.reshape(-1, step) >> 14
    span = jnp.stack([by_step[:, 0], by_step[:, -1]])
    spec = forward(got, coef, cells, span, planes, step)

    wins = spec.shape[1]
    width = planes // wins
    modes = M // bricks
    kz = M // pair
    sent = spec.reshape(2, wins, chans, bricks, modes, pair, width * kz)
    sent = sent.transpose(3, 5, 0, 1, 4, 2, 6).reshape(bricks * pair, 2, wins, modes, chans, width * kz)
    pencil = lax.all_to_all(sent, both, split_axis=0, concat_axis=0, tiled=True)
    pencil = pencil.reshape(bricks, pair, 2, wins, modes, chans, width, kz)
    pencil = pencil.transpose(4, 1, 5, 7, 2, 0, 3, 6).reshape(modes, C, kz, 2 * G)

    scale = 1.0 / (G * math.sqrt(G))
    x_cos, x_sin = angles(M, True)
    x_cos, x_sin = x_cos.T, x_sin.T
    ahead = np.stack([np.concatenate([x_cos, x_sin]), np.concatenate([-x_sin, x_cos])])
    ahead = jnp.asarray(ahead.astype(BF16))
    coeff = jnp.einsum("bikx,rxa->rbika", pencil, ahead, preferred_element_type=F32) * scale
    coeff = coeff.reshape(2, modes, C, kz * M)
    c_real, c_imag = coeff[0], coeff[1]
    w_real, w_imag = spectral_weight[0], spectral_weight[1]
    m_real = jnp.sum(w_real * c_real[:, :, None] - w_imag * c_imag[:, :, None], axis=1)
    m_imag = jnp.sum(w_real * c_imag[:, :, None] + w_imag * c_real[:, :, None], axis=1)
    mixed = jnp.stack([m_real, m_imag]).astype(BF16).reshape(2, modes, C, kz, M)
    back = np.stack([np.stack([x_cos, -x_sin]), np.stack([x_sin, x_cos])])
    back = jnp.asarray(back.astype(BF16))
    lines = jnp.einsum("sboka,rsxa->rbokx", mixed, back, preferred_element_type=F32).astype(BF16)
    lines = lines.reshape(2, modes, pair, chans, kz, bricks, planes)
    lines = lines.transpose(5, 2, 0, 1, 3, 4, 6).reshape(bricks * pair, 2, modes, chans, kz * planes)
    lines = lax.all_to_all(lines, both, split_axis=0, concat_axis=0, tiled=True)
    lines = lines.reshape(bricks, pair, 2, modes, chans, kz, planes)
    wide = min(4, planes)
    lines = lines.reshape(bricks, pair, 2, modes, chans, kz, planes // wide, wide)
    lines = lines.transpose(2, 6, 4, 0, 3, 7, 1, 5).reshape(2, planes // wide, chans, M, wide, M)
    r_real, r_imag = lines[0], lines[1]
    top = jnp.stack([r_real, -r_imag], axis=4)
    low = jnp.stack([-r_imag, -r_real], axis=4)
    mat = jnp.stack([top, low], axis=2).reshape(planes // wide, chans * 2 * M, wide * 2 * M)

    skip = skip_at(every, coef, cells, skip_weight, bricks, slots, slab_cells)
    hidden = inverse(cells, skip, bias, mat, span, planes, step)
    answered = lax.all_to_all(
        hidden.reshape(chans, bricks, slots), "brick", split_axis=1, concat_axis=1, tiled=True
    )
    return decode(answered.reshape(chans, -1), dec.reshape(1, -1), points, point_count)


def solution(mesh):
    return jax.shard_map(
        shards,
        mesh=mesh,
        in_specs=(
            P("chan", ("groups", "brick")),
            P(("groups", "brick"), None),
            P(("groups", "brick"), None, None),
            P(("groups", "brick"), None, None),
            P(("groups", "brick"), None, None),
            P(("groups", "brick"), None, None),
            P("chan", None),
            P(None, "brick", None, None, "chan"),
            P("chan"),
        ),
        out_specs=P("chan", ("groups", "brick")),
        check_vma=False,
    )
```

time: 1780 us -> 546 us (0.31)
  matrix products: 661 us -> 0.92 us
  local copies, waits for them, and re-layouts: 561 us -> 186 us
  other arithmetic: 374 us -> 40.6 us
  Pallas kernels: 0 us -> 183 us
  blocking collectives: 64.4 us -> 0 us
  starting transfers between devices: 21.7 us -> 70.9 us
  waiting for transfers between devices: 81.5 us -> 45.1 us
    dot_general x21 -> x2, matrix products: 661 us -> 0.92 us  [the longest x1 0.49 us: shards(): jnp.einsum('sboka,rsxa->rbokx', mixed, back, preferred_element_type=F32)]
    scatter-add x4 -> x0, other arithmetic: 332 us -> none  [the longest x3 245 us: shards(): jnp.zeros((chans, slab_cells), jnp.float32).at[:, cells_in]]
    gather x2 -> x0, local copies, waits for them, and re-layouts: 301 us -> none  [the longest x1 243 us: shards(): requested = hidden[:, cells_in].reshape(chans, bricks, slots)]
    pallas_call x0 -> x5, Pallas kernels: none -> 183 us  [the longest x1 90.8 us: skip_at(): pl.pallas_call(lambda *r: skip_kernel(lists, per, wide, *r), grid_spec=pl...]
    scatter-add x3 -> x0, local copies, waits for them, and re-layouts: 71.2 us -> none  [the longest x2 70.2 us: shards(): jnp.zeros((chans, slab_cells), jnp.float32).at[:, cells_in]]
    reshape x5 -> x16, local copies, waits for them, and re-layouts: 10.1 us -> 79.3 us  [the longest x1 21.3 us: shards(): jnp.stack([top, low], axis=2)]
    all_to_all x3 -> x0, blocking collectives: 64.4 us -> none  [the longest x1 52.7 us: shards(): lax.all_to_all(partial_spec, 'brick', split_axis=3, concat_axis=2, tiled=...]
    all_to_all x4 -> x5, starting transfers between devices: 21.7 us -> 70.7 us  [the longest x1 32.9 us: shards(): lax.all_to_all(hidden.reshape(chans, bricks, slots), 'brick', split_axis=...]
  transfers between devices with their start and end apart: 5 -> 6, of which waited for: 3 -> 3; matrix products, arithmetic and copies ran while one was open for 48% -> 18% of each run, Pallas kernels for 0% -> 18%
where the time goes in v1:
time: 546 us; the launch traced here: 540 us
  local copies, waits for them, and re-layouts  186 us (34%)
  Pallas kernels  183 us (34%)
  starting transfers between devices  70.9 us (13%)
  waiting for transfers between devices  45.1 us (8%)
  other arithmetic  40.6 us (7%)
  between operations  13.8 us (3%)
    pallas_call x1, Pallas kernels, skip_at(): pl.pallas_call(lambda *r: skip_kernel(lists, per, wide, *r), grid_spec=pl...  90.8 us
    pallas_call x1, Pallas kernels, inverse(): pl.pallas_call(lambda *r: inverse_kernel(chans, width, wins, *r), grid_sp...  42.1 us
    pallas_call x1, Pallas kernels, forward(): pl.pallas_call(lambda *r: forward_kernel(chans, width, wins, *r), grid_sp...  35.8 us
    all_to_all x1, starting transfers between devices, shards(): lax.all_to_all(hidden.reshape(chans, bricks, slots), 'brick', split_axis=...  32.9 us
    transpose x1, local copies, waits for them, and re-layouts, shards(): pencil.transpose(4, 1, 5, 7, 2, 0, 3, 6).reshape(modes, C, kz, 2 * G)  26.2 us
    neg x2, local copies, waits for them, and re-layouts, shards(): top = jnp.stack([r_real, -r_imag], axis=4)  21.5 us
    reshape x1, local copies, waits for them, and re-layouts, shards(): jnp.stack([top, low], axis=2)  21.3 us
    reshape x2, local copies, waits for them, and re-layouts, shards(): pencil.transpose(4, 1, 5, 7, 2, 0, 3, 6).reshape(modes, C, kz, 2 * G)  18.1 us
  transfers between devices with their start and end apart: 6, of which 3 were waited for; matrix products, arithmetic and copies ran while one was open for 18% of the time, Pallas kernels for 18%

profile of v1, /device:TPU:0, one launch (start us, length us, event | category | flops | bytes accessed | tf_op | source)
XLA Modules:
  0.0 540.3 jit_solution(8196024071921541619)
XLA Ops:
  6.5 1.6 bitcast_select_fusion.2
  8.1 1.6 bitcast_select_fusion
  9.7 7.8 %sort.29.cloned.1.call-done = (s32[8,2048]{1,0:T(8,128)}, s32[8,2048]{1,0:T(8,128)}, f32[8,2048]{1,0:T(8,128)}, f32[8,2048]{1,0:T(8,128)}) async-done(((s32[8,2048]{1,0:T(8,128)}, s32[8,2048]{1,0:T(8,128)}, f32[8,2048]{1,0:T(8,128)}, f32[8,2048]{1,0:T(8,128)}), (s32[8,2048]{1,0:T(8,128)}, s32[8,2048]{1,0:T(8,128)}, f32[8,2048]{1,0:T(8,128)}, f32[8,2048]{1,0:T(8,128)})) %sort.29.cloned.1.call-update) | async-done | bytes 262160 | tf_op jit(solution)/shard_map/sort | solution.py:329
  17.5 0.8 convert_element_type.55
  18.4 0.9 stack.47
  19.3 0.8 pad_maximum_fusion.1
  20.1 7.2 %all-to-all-start = ((f32[8,2,2048]{2,1,0:T(2,128)}), f32[8,2,2048]{2,1,0:T(2,128)S(1)}, u32[]{:S(2)}, u32[]{:S(2)}) async-start(f32[8,2,2048]{2,1,0:T(2,128)} %pad_maximum_fusion.1), calls=%async_computation | async-start | bytes 262144 | tf_op jit(solution)/shard_map/all_to_all | solution.py:336
  27.3 0.9 reshape.172.r_0_
  28.2 0.9 copy.92
  29.1 6.0 %shard_map.145 = bf16[16,16384]{1,0:T(8,128)(2,1)S(1)} custom-call(bf16[256,128]{1,0:T(8,128)(2,1)S(1)} %reshape.172.r_0_, s32[1,16384]{1,0:T(1,128)S(1)} %bitcast.137), custom_call_target="tpu_custom_call" | custom-call | tf_op jit(solution)/shard_map/pallas_call | solution.py:54
  35.1 0.8 copy.100
  36.0 6.0 %all-to-all-start.1 = ((bf16[16,8,2048]{2,0,1:T(8,128)(2,1)}), bf16[16,8,2048]{2,0,1:T(8,128)(2,1)S(1)}, u32[]{:S(2)}, u32[]{:S(2)}) async-start(bf16[16,8,2048]{2,0,1:T(8,128)(2,1)} %bitcast.125), calls=%async_computation.1 | async-start | bytes 1048576 | tf_op jit(solution)/shard_map/all_to_all | solution.py:339
  42.5 13.5 %all-to-all-done.1 = bf16[16,8,2048]{2,0,1:T(8,128)(2,1)S(1)} async-done(((bf16[16,8,2048]{2,0,1:T(8,128)(2,1)}), bf16[16,8,2048]{2,0,1:T(8,128)(2,1)S(1)}, u32[]{:S(2)}, u32[]{:S(2)}) %all-to-all-start.1) | async-done | bytes 524320 | tf_op jit(solution)/shard_map/all_to_all | solution.py:339
  56.0 35.8 %shard_map.147 = bf16[2,2,16,32,256]{4,3,2,1,0:T(8,128)(2,1)S(1)} custom-call(s32[2,64]{1,0:T(2,128)S(1)} %pad_add_fusion.1.r_0_, bf16[16,16384]{1,0:T(8,128)(2,1)S(1)} %bitcast.126, f32[1,16384]{1,0:T(1,128)S(1)} %bitcast.139, s32[1,16384]{1,0:T(1,128)S(1)} %bitcast.128, bf16[128,128]{1,0:T(8,128)(2,1)S(1)} %copy-done.1, bf16[64,128]{1,0:T(8,128)(2,1)S(1)} %copy-done.3), custom_call_target="tpu_custom_call" | custom-call | tf_op jit(solution)/shard_map/pallas_call | solution.py:123
  92.1 1.7 copy.69
  93.8 17.7 %all-to-all-start.2 = ((bf16[16,2,2,4,16,128]{5,4,3,2,1,0:T(8,128)(2,1)}), bf16[16,2,2,4,16,128]{5,4,3,2,1,0:T(8,128)(2,1)S(1)}, u32[]{:S(2)}, u32[]{:S(2)}) async-start(bf16[16,2,2,4,16,128]{5,4,3,2,1,0:T(8,128)(2,1)} %bitcast.17), calls=%async_computation.2 | async-start | bytes 2097152 | tf_op jit(solution)/shard_map/all_to_all | solution.py:354
  112.7 4.9 copy.68.r_2_
  117.6 16.9 %all-to-all-done.2 = bf16[16,2,2,4,16,128]{5,4,3,2,1,0:T(8,128)(2,1)S(1)} async-done(((bf16[16,2,2,4,16,128]{5,4,3,2,1,0:T(8,128)(2,1)}), bf16[16,2,2,4,16,128]{5,4,3,2,1,0:T(8,128)(2,1)S(1)}, u32[]{:S(2)}, u32[]{:S(2)}) %all-to-all-start.2) | async-done | bytes 1048608 | tf_op jit(solution)/shard_map/all_to_all | solution.py:354
  134.5 7.3 %reshape.179 = bf16[8,2,2,2,4,16,8,16]{7,6,5,4,3,2,1,0:T(8,128)(2,1)} reshape(bf16[16,2,2,4,16,128]{5,4,3,2,1,0:T(8,128)(2,1)S(1)} %all-to-all-done.2) | data formatting | bytes 2097152 | tf_op jit(solution)/shard_map/reshape | solution.py:355
  141.9 26.2 %copy.70 = bf16[4,2,16,16,2,8,2,8]{2,1,7,6,5,4,3,0:T(2,128)(2,1)} copy(bf16[4,2,16,16,2,8,2,8]{3,7,2,0,6,4,1,5:T(8,128)(2,1)} %bitcast.143) | data formatting | bytes 2097152 | tf_op jit(solution)/shard_map/transpose | solution.py:356
  168.0 14.2 %reshape.180 = bf16[4,32,16,256]{1,3,2,0:T(8,128)(2,1)} reshape(bf16[4,2,16,16,2,8,2,8]{2,1,7,6,5,4,3,0:T(2,128)(2,1)} %copy.70) | data formatting | bytes 2097152 | tf_op jit(solution)/shard_map/reshape | solution.py:356
  182.2 3.9 copy.80
  187.6 7.5 %fusion.1 = (bf16[4,32,512]{2,1,0:T(8,128)(2,1)S(1)}, bf16[4,32,512]{2,1,0:T(8,128)(2,1)S(1)}) fusion(f32[2,4,32,32,512]{4,3,2,1,0:T(8,128)} %param.22, f32[4,32,512]{2,1,0:T(8,128)S(1)} %mul.60, f32[4,32,512]{2,1,0:T(8,128)S(1)} %mul.57), kind=kLoop, calls=%fused_computation.4 | loop fusion | flops 16646144 | bytes 17563648 | tf_op jit(solution)/shard_map/reduce_sum | solution.py:367
  195.7 0.5 fusion.5
  196.2 7.3 %reshape.181 = bf16[2,4,2,16,16,8,16]{6,5,4,0,3,2,1:T(8,128)(2,1)} reshape(bf16[2,4,32,16,128]{4,3,0,2,1:T(8,128)(2,1)S(1)} %fusion.5) | data formatting | bytes 2097152 | tf_op jit(solution)/shard_map/reshape | solution.py:373
  203.6 8.8 %copy.98 = bf16[2,4,2,16,16,8,16]{6,4,3,1,0,2,5:T(8,128)(2,1)} copy(bf16[2,4,2,16,16,8,16]{6,5,4,0,3,2,1:T(8,128)(2,1)} %reshape.181) | data formatting | bytes 2097152 | tf_op jit(solution)/shard_map/reshape | solution.py:373
  212.4 11.0 %reshape.182 = bf16[16,2,4,16,256]{4,3,2,1,0:T(8,128)(2,1)} reshape(bf16[8,2,2,4,16,16,16]{6,5,4,3,2,1,0:T(8,128)(2,1)} %bitcast.144) | data formatting | bytes 2097152 | tf_op jit(solution)/shard_map/reshape | solution.py:374
  223.4 6.9 %all-to-all-start.3 = ((bf16[16,2,4,16,256]{4,3,2,1,0:T(8,128)(2,1)}), bf16[16,2,4,16,256]{4,3,2,1,0:T(8,128)(2,1)S(1)}, u32[]{:S(2)}, u32[]{:S(2)}) async-start(bf16[16,2,4,16,256]{4,3,2,1,0:T(8,128)(2,1)} %reshape.182), calls=%async_computation.3 | async-start | bytes 2097152 | tf_op jit(solution)/shard_map/all_to_all | solution.py:375
  230.3 1.6 reduce-precision_convert_fusion
  231.9 0.6 bitcast_bitcast_fusion.r_4_
  232.5 90.8 %shard_map.146.r_2_ = f32[16,16384]{1,0:T(8,128)S(1)} custom-call(s32[128,16]{1,0:T(8,128)S(1)} %copy.67.r_0_, s32[128]{0:T(128)S(1)} %fusion.10.r_1_, s32[16384,1]{1,0:T(8,128)} %copy.68.r_2_, s32[128,128]{1,0:T(8,128)S(1)} %bitcast.132, bf16[128,64,128]{2,1,0:T(8,128)(2,1)S(1)} %bitcast_bitcast_fusion.r_4_, f32[16,32]{1,0:T(8,128)S(1)} %copy-done.4), custom_call_target="tpu_custom_call" | custom-call | tf_op jit(solution)/shard_map/pallas_call | solution.py:189
  323.3 5.8 %copy.73 = bf16[16,2,4,16,256]{3,4,2,1,0:T(8,128)(2,1)} copy(bf16[16,2,4,16,256]{4,3,2,1,0:T(8,128)(2,1)S(1)} %all-to-all-done.3) | data formatting | bytes 2097152 | tf_op jit(solution)/shard_map/all_to_all | solution.py:375
  329.1 8.3 %slice_negate_fusion = (bf16[1,4,16,8,4,4,2,16]{2,5,1,7,4,0,6,3:T(4,128)(2,1)}, bf16[1,4,16,8,4,4,2,16]{2,5,1,7,4,0,6,3:T(4,128)(2,1)}) fusion(bf16[2,4,16,8,4,4,2,16]{2,5,1,7,4,0,6,3:T(4,128)(2,1)} %bitcast.142), kind=kLoop, calls=%fused_computation.10 | loop fusion | flops 262144 | bytes 2097152 | tf_op jit(solution)/shard_map/neg | solution.py:381
  337.5 13.7 %copy.74 = bf16[1,4,16,8,4,4,2,16]{7,6,4,3,5,2,1,0:T(2,128)(2,1)} copy(bf16[1,4,16,8,4,4,2,16]{2,5,1,7,4,0,6,3:T(4,128)(2,1)} %get-tuple-element.21) | data formatting | bytes 1048576 | tf_op jit(solution)/shard_map/slice | solution.py:380
  351.2 6.8 %stack_squeeze.11 = bf16[4,16,32,4,1,32]{5,2,3,1,0,4:T(8,128)(2,1)S(1)} reshape(bf16[1,4,16,8,4,4,2,16]{7,6,4,3,5,2,1,0:T(2,128)(2,1)} %copy.74) | data formatting | bytes 1048576 | tf_op jit(solution)/shard_map/stack;squeeze | solution.py:381
  358.0 1.9 neg.26
  359.9 13.7 %copy.75 = bf16[1,4,16,8,4,4,2,16]{7,6,4,3,5,2,1,0:T(2,128)(2,1)} copy(bf16[1,4,16,8,4,4,2,16]{2,5,1,7,4,0,6,3:T(4,128)(2,1)} %get-tuple-element.20) | data formatting | bytes 1048576 | tf_op jit(solution)/shard_map/neg | solution.py:381
  373.7 7.8 %neg.25 = bf16[4,16,32,4,1,32]{5,2,3,1,0,4:T(8,128)(2,1)} reshape(bf16[1,4,16,8,4,4,2,16]{7,6,4,3,5,2,1,0:T(2,128)(2,1)} %copy.75) | data formatting | bytes 1048576 | tf_op jit(solution)/shard_map/neg | solution.py:381
  381.4 6.5 %maximum_bitcast_fusion = (bf16[4,16,1,32,4,2,32]{6,3,4,1,0,5,2:T(8,128)(2,1)}, bf16[4,16,1,32,4,2,32]{6,3,4,1,0,5,2:T(8,128)(2,1)}) fusion(bf16[4,16,32,4,1,32]{5,2,3,1,0,4:T(8,128)(2,1)} %neg.25, bf16[4,16,32,4,1,32]{5,2,3,1,0,4:T(8,128)(2,1)S(1)} %stack_squeeze.11, bf16[4,16,32,4,1,32]{5,2,3,1,0,4:T(8,128)(2,1)} %neg.26), kind=kLoop, calls=%fused_computation.11 | loop fusion | flops 1048576 | bytes 3670016 | tf_op jit(solution)/shard_map/stack | solution.py:383
  387.9 8.6 %pad_maximum_fusion = bf16[4,16,2,32,4,2,32]{6,3,4,1,0,5,2:T(8,128)(2,1)} fusion(bf16[4,16,1,32,4,2,32]{6,3,4,1,0,5,2:T(8,128)(2,1)} %get-tuple-element.23, bf16[4,16,1,32,4,2,32]{6,3,4,1,0,5,2:T(8,128)(2,1)} %get-tuple-element.22), kind=kLoop, calls=%fused_computation | loop fusion | flops 1048576 | bytes 4194304 | tf_op jit(solution)/shard_map/stack | solution.py:383
  396.5 16.4 %copy.76 = bf16[4,16,2,32,4,2,32]{6,5,4,3,2,1,0:T(2,128)(2,1)} copy(bf16[4,16,2,32,4,2,32]{6,3,4,1,0,5,2:T(8,128)(2,1)} %pad_maximum_fusion) | data formatting | bytes 4194304 | tf_op jit(solution)/shard_map/stack | solution.py:383
  412.9 21.3 %reshape.183.r_4_ = bf16[4,1024,256]{2,1,0:T(8,128)(2,1)S(1)} reshape(bf16[4,16,2,32,4,2,32]{6,5,4,3,2,1,0:T(2,128)(2,1)} %copy.76) | data formatting | bytes 4194304 | tf_op jit(solution)/shard_map/reshape | solution.py:383
  434.3 42.1 %shard_map.148 = bf16[16,16384]{1,0:T(8,128)(2,1)S(1)} custom-call(s32[2,64]{1,0:T(2,128)S(1)} %pad_add_fusion.1.r_0_, s32[1,16384]{1,0:T(1,128)S(1)} %bitcast.133, f32[16,16384]{1,0:T(8,128)S(1)} %shard_map.146.r_2_, f32[16,1]{1,0:T(8,128)S(1)} %copy.77.r_3_, bf16[4,1024,256]{2,1,0:T(8,128)(2,1)S(1)} %reshape.183.r_4_, bf16[128,128]{1,0:T(8,128)(2,1)S(1)} %copy-done.1, ...), custom_call_target="tpu_custom_call" | custom-call | tf_op jit(solution)/shard_map/pallas_call | solution.py:247
  476.4 0.8 copy.99
  477.2 32.9 %all-to-all-start.4 = ((bf16[16,8,2048]{2,0,1:T(8,128)(2,1)}), bf16[16,8,2048]{2,0,1:T(8,128)(2,1)S(1)}, u32[]{:S(2)}, u32[]{:S(2)}) async-start(bf16[16,8,2048]{2,0,1:T(8,128)(2,1)} %bitcast.124), calls=%async_computation.4 | async-start | bytes 1048576 | tf_op jit(solution)/shard_map/all_to_all | solution.py:387
  510.2 14.7 %all-to-all-done.4 = bf16[16,8,2048]{2,0,1:T(8,128)(2,1)S(1)} async-done(((bf16[16,8,2048]{2,0,1:T(8,128)(2,1)}), bf16[16,8,2048]{2,0,1:T(8,128)(2,1)S(1)}, u32[]{:S(2)}, u32[]{:S(2)}) %all-to-all-start.4) | async-done | bytes 524320 | tf_op jit(solution)/shard_map/all_to_all | solution.py:387
  524.9 7.9 %shard_map.149 = f32[256,128]{1,0:T(8,128)S(1)} custom-call(bf16[16,16384]{1,0:T(8,128)(2,1)S(1)} %bitcast.135, f32[1,16384]{1,0:T(1,128)S(1)} %bitcast.141, s32[1,16384]{1,0:T(1,128)S(1)} %bitcast.138), custom_call_target="tpu_custom_call" | custom-call | tf_op jit(solution)/shard_map/pallas_call | solution.py:290
  532.8 0.7 reshape.187
  (52 shorter events, 4.2 us)
Async XLA Ops:
  6.5 49.5 %copy-start.1 = (bf16[128,128]{1,0:T(8,128)(2,1)S(1)}, bf16[128,128]{1,0:T(8,128)(2,1)}, u32[]{:S(2)}) copy-start(bf16[128,128]{1,0:T(8,128)(2,1)} %constant.42.clone.r_4_.r_5_) | copy-start | bytes 98308
  6.5 49.5 %copy-start.3 = (bf16[64,128]{1,0:T(8,128)(2,1)S(1)}, bf16[64,128]{1,0:T(8,128)(2,1)}, u32[]{:S(2)}) copy-start(bf16[64,128]{1,0:T(8,128)(2,1)} %constant.43.clone.r_5_) | copy-start | bytes 49156
  6.5 11.0 %sort.29.cloned.1.call-start = ((), (), s32[]{:S(2)}) async-start(), calls=%async_computation.6 | async-start | bytes 786464 | tf_op jit(solution)/shard_map/sort | solution.py:329
  20.1 15.9 %all-to-all-start = ((f32[8,2,2048]{2,1,0:T(2,128)}), f32[8,2,2048]{2,1,0:T(2,128)S(1)}, u32[]{:S(2)}, u32[]{:S(2)}) async-start(f32[8,2,2048]{2,1,0:T(2,128)} %pad_maximum_fusion.1), calls=%async_computation | async-start | bytes 262144 | tf_op jit(solution)/shard_map/all_to_all | solution.py:336
  36.0 20.0 %all-to-all-start.1 = ((bf16[16,8,2048]{2,0,1:T(8,128)(2,1)}), bf16[16,8,2048]{2,0,1:T(8,128)(2,1)S(1)}, u32[]{:S(2)}, u32[]{:S(2)}) async-start(bf16[16,8,2048]{2,0,1:T(8,128)(2,1)} %bitcast.125), calls=%async_computation.1 | async-start | bytes 1048576 | tf_op jit(solution)/shard_map/all_to_all | solution.py:339
  56.0 56.7 %copy-start = (bf16[8,2,8,2048]{3,2,0,1:T(8,128)(2,1)}, bf16[8,2,8,2048]{3,2,0,1:T(8,128)(2,1)S(1)}, u32[]{:S(2)}) copy-start(bf16[8,2,8,2048]{3,2,0,1:T(8,128)(2,1)S(1)} %copy.90) | copy-start | bytes 1572868
  56.0 55.8 %copy-start.7 = (f32[16]{0:T(128)S(1)}, f32[16]{0:T(128)}, u32[]{:S(2)}) copy-start(f32[16]{0:T(128)} %param.23) | copy-start | bytes 196
  93.8 40.7 %all-to-all-start.2 = ((bf16[16,2,2,4,16,128]{5,4,3,2,1,0:T(8,128)(2,1)}), bf16[16,2,2,4,16,128]{5,4,3,2,1,0:T(8,128)(2,1)S(1)}, u32[]{:S(2)}, u32[]{:S(2)}) async-start(bf16[16,2,2,4,16,128]{5,4,3,2,1,0:T(8,128)(2,1)} %bitcast.17), calls=%async_computation.2 | async-start | bytes 2097152 | tf_op jit(solution)/shard_map/all_to_all | solution.py:354
  111.6 118.7 %all-gather.2.cloned.1.call-start = ((), (), s32[]{:S(2)}) async-start(), calls=%async_computation.5 | async-start | bytes 1572864 | tf_op jit(solution)/shard_map/all_gather | solution.py:342
  182.2 3.9 copy-start.6
  187.6 8.1 %copy-start.8 = (bf16[2,2,128,32,1,1]{2,3,1,0,5,4:T(8,128)(2,1)S(1)}, bf16[2,2,128,32,1,1]{2,3,1,0,5,4:T(8,128)(2,1)}, u32[]{:S(2)}) copy-start(bf16[2,2,128,32,1,1]{2,3,1,0,5,4:T(8,128)(2,1)} %constant.54) | copy-start | bytes 98308
  223.4 99.9 %all-to-all-start.3 = ((bf16[16,2,4,16,256]{4,3,2,1,0:T(8,128)(2,1)}), bf16[16,2,4,16,256]{4,3,2,1,0:T(8,128)(2,1)S(1)}, u32[]{:S(2)}, u32[]{:S(2)}) async-start(bf16[16,2,4,16,256]{4,3,2,1,0:T(8,128)(2,1)} %reshape.182), calls=%async_computation.3 | async-start | bytes 2097152 | tf_op jit(solution)/shard_map/all_to_all | solution.py:375
  230.3 2.2 copy-start.4
  412.9 21.3 %copy-start.2 = (bf16[64,128]{1,0:T(8,128)(2,1)S(1)}, bf16[64,128]{1,0:T(8,128)(2,1)}, u32[]{:S(2)}) copy-start(bf16[64,128]{1,0:T(8,128)(2,1)} %constant.46.clone.r_6_) | copy-start | bytes 49156
  434.2 75.8 %copy-start.5 = (f32[8,2048]{1,0:T(8,128)S(1)}, f32[8,2048]{1,0:T(8,128)}, u32[]{:S(2)}) copy-start(f32[8,2048]{1,0:T(8,128)} %get-tuple-element.12) | copy-start | bytes 196612
  477.2 47.7 %all-to-all-start.4 = ((bf16[16,8,2048]{2,0,1:T(8,128)(2,1)}), bf16[16,8,2048]{2,0,1:T(8,128)(2,1)S(1)}, u32[]{:S(2)}, u32[]{:S(2)}) async-start(bf16[16,8,2048]{2,0,1:T(8,128)(2,1)} %bitcast.124), calls=%async_computation.4 | async-start | bytes 1048576 | tf_op jit(solution)/shard_map/all_to_all | solution.py:387
Sparse Core Ops, SparseCore 0:
  9.9 7.3 sort.31.cloned.1.call-done
  117.8 10.2 all-gather.1
  (1 shorter events, 0.0 us)

commit v2 on v1

--- a/solution.py
+++ b/solution.py
@@ -140,74 +140,191 @@
     )(span, feats, coef, cells, ytab, ztab)
 
 
-def skip_kernel(lists, per, wide, bounds_ref, rounds_ref, mine_ref, cells_ref, vals_ref, w_ref, out_ref):
-    step = pl.program_id(0)
+def skip_kernel(chans, group, count_ref, work_ref, mine_ref, cells_ref, vals_ref, out_ref):
+    live = count_ref[pl.program_id(0)]
     mine = mine_ref[...]
-    lanes = 128
 
     def one(turn, acc):
         hits = []
         vals = []
-        for src in range(lists):
-            for off in range(wide):
-                at = bounds_ref[step, 2 * src] + turn * wide + off
-                live = at < bounds_ref[step, 2 * src + 1]
-                row = src * per + jnp.where(live, at, 0)
-                other = jnp.where(live, cells_ref[pl.ds(row, 1), :], -1)
-                hits.append(jnp.where(mine == other, 1.0, 0.0).astype(BF16))
-                vals.append(vals_ref[row])
+        for off in range(group):
+            at = turn * group + off
+            row = work_ref[0, 0, at]
+            other = jnp.where(at < live, cells_ref[pl.ds(row, 1), :], -1)
+            hits.append(jnp.where(mine == other, 1.0, 0.0).astype(BF16))
+            vals.append(vals_ref[row])
         hit = jnp.concatenate(hits, axis=1)
-        val = jnp.concatenate(vals, axis=1)
-        return acc + lax.dot_general(val, hit, NT, preferred_element_type=F32)
-
-    acc = lax.fori_loop(0, rounds_ref[step], one, jnp.zeros((2 * C, lanes), F32))
-    latent = acc[:C] + acc[C:]
-    out_ref[...] = jnp.dot(
-        w_ref[...], latent, precision=lax.Precision.HIGHEST, preferred_element_type=F32
-    )
-
-
-def skip_at(feats, coef, cells, weight, lists, slots, slab_cells, wide=2):
+        val = jnp.concatenate(vals, axis=0)
+        return acc + mm(hit, val)
+
+    rounds = (live + group - 1) // group
+    acc = lax.fori_loop(0, rounds, one, jnp.zeros((128, 2 * chans), F32))
+    rows = lax.broadcasted_iota(jnp.int32, (chans, 2 * chans), 0)
+    cols = lax.broadcasted_iota(jnp.int32, (chans, 2 * chans), 1)
+    fold = jnp.where((cols == rows) | (cols == rows + chans), 1.0, 0.0)
+    out_ref[...] = lax.dot_general(
+        fold, acc, NT, precision=lax.Precision.HIGHEST, preferred_element_type=F32
+    )
+
+
+def skip_at(feats, coef, cells, weight, slab_cells, group=8):
+    chans = weight.shape[0]
     total = cells.shape[1]
-    per = slots // 128
     chunks = total // 128
-    vals = feats.astype(F32) * coef
+    vals = jnp.einsum(
+        "in,oi->no",
+        feats.astype(F32) * coef,
+        weight,
+        precision=lax.Precision.HIGHEST,
+        preferred_element_type=F32,
+    )
     hi = lax.reduce_precision(vals, 8, 7)
-    lo = (vals - hi).astype(BF16)
-    both = jnp.concatenate([hi.astype(BF16), lo], axis=0)
-    both = both.reshape(2 * C, chunks, 128).transpose(1, 0, 2)
+    both = jnp.concatenate([hi, vals - hi], axis=1).astype(BF16).reshape(chunks, 128, 2 * chans)
     rows = cells.reshape(chunks, 128)
     low = rows[:, 0]
-    high = jnp.minimum(rows[:, 127], slab_cells - 1)
-    q_low = low.reshape(1, lists, per)
-    q_high = rows[:, 127].reshape(1, lists, per)
-    start = jnp.sum((q_high < low[:, None, None]).astype(jnp.int32), axis=2)
-    end = jnp.sum((q_low <= high[:, None, None]).astype(jnp.int32), axis=2)
-    end = jnp.where(low[:, None] >= slab_cells, start, jnp.maximum(end, start))
-    rounds = jnp.max((end - start + wide - 1) // wide, axis=1)
-    bounds = jnp.stack([start, end], axis=2).reshape(chunks, 2 * lists)
+    top = rows[:, 127]
+    high = jnp.minimum(top, slab_cells - 1)
+    meets = (top[None] >= low[:, None]) & (low[None] <= high[:, None])
+    meets &= low[:, None] < slab_cells
+    places = jnp.arange(chunks, dtype=jnp.int32)
+    work = lax.sort(jnp.where(meets, places[None], chunks - 1), dimension=1)
+    count = jnp.sum(meets.astype(jnp.int32), axis=1)
     return pl.pallas_call(
-        lambda *r: skip_kernel(lists, per, wide, *r),
+        lambda *r: skip_kernel(chans, group, *r),
         grid_spec=pltpu.PrefetchScalarGridSpec(
-            num_scalar_prefetch=2,
+            num_scalar_prefetch=1,
             grid=(chunks,),
             in_specs=[
-                pl.BlockSpec((128, 1), lambda i, a, b: (i, 0)),
-                pl.BlockSpec((chunks, 128), lambda i, a, b: (0, 0)),
-                pl.BlockSpec((chunks, 2 * C, 128), lambda i, a, b: (0, 0, 0)),
-                pl.BlockSpec(weight.shape, lambda i, a, b: (0, 0)),
+                pl.BlockSpec((1, 1, chunks), lambda i, a: (i, 0, 0), memory_space=pltpu.SMEM),
+                pl.BlockSpec((128, 1), lambda i, a: (i, 0)),
+                pl.BlockSpec((chunks, 128), lambda i, a: (0, 0)),
+                pl.BlockSpec((chunks, 128, 2 * chans), lambda i, a: (0, 0, 0)),
             ],
-            out_specs=pl.BlockSpec((weight.shape[0], 128), lambda i, a, b: (0, i)),
+            out_specs=pl.BlockSpec((chans, 128), lambda i, a: (0, i)),
         ),
-        out_shape=jax.ShapeDtypeStruct((weight.shape[0], total), F32),
-        compiler_params=params(),
-    )(bounds, rounds, cells.reshape(total, 1), rows, both, weight)
-
-
-def inverse_kernel(chans, width, wins, span_ref, cell_ref, skip_ref, bias_ref, r_ref, ytab_ref, ztab_ref, out_ref, acc_ref):
+        out_shape=jax.ShapeDtypeStruct((chans, total), F32),
+        compiler_params=params(),
+    )(count, work.reshape(chunks, 1, chunks), cells.reshape(total, 1), rows, both)
+
+
+def ahead_kernel(pair, wins, in_ref, mat_ref, out_ref, acc_ref):
+    step = pl.program_id(0)
+    _, _, _, _, modes, chans, lanes = in_ref.shape
+    rows = []
+    for src in range(pair):
+        parts = [
+            in_ref[0, src, s, win].reshape(modes * chans, lanes) for s in range(2) for win in range(wins)
+        ]
+        rows.append(jnp.concatenate(parts, axis=1))
+    part = mm(jnp.concatenate(rows, axis=0), mat_ref[0])
+
+    @pl.when(step == 0)
+    def _():
+        acc_ref[...] = part
+
+    @pl.when(step > 0)
+    def _():
+        acc_ref[...] += part
+
+    @pl.when(step == pl.num_programs(0) - 1)
+    def _():
+        half = acc_ref.shape[1] // 2
+        full = acc_ref[...] * (1.0 / (G * math.sqrt(G)))
+        full = full.reshape(pair, modes, chans, 2 * half)
+        for src in range(pair):
+            for s in range(2):
+                out_ref[s, :, src * chans : (src + 1) * chans, :] = full[
+                    src, :, :, s * half : (s + 1) * half
+                ]
+
+
+def x_matrices(bricks, kz):
+    planes = G // bricks
+    x_cos, x_sin = angles(M, True)
+    x_cos = x_cos.reshape(M, bricks, planes)
+    x_sin = x_sin.reshape(M, bricks, planes)
+    eye = np.eye(kz)
+    ahead = np.zeros((bricks, 2, planes, kz, 2, kz, M), np.float32)
+    back = np.zeros((bricks, 2, kz, M, 2, planes, kz), np.float32)
+    for s, r, table in ((0, 0, x_cos), (1, 0, x_sin), (0, 1, -x_sin), (1, 1, x_cos)):
+        ahead[:, s, :, :, r] = np.einsum("aBx,kq->Bxkqa", table, eye)
+        back[:, r, :, :, s] = np.einsum("aBx,kq->Bkaxq", table, eye)
+    side = 2 * planes * kz
+    return (
+        jnp.asarray(ahead.reshape(bricks, side, 2 * kz * M).astype(BF16)),
+        jnp.asarray(back.reshape(bricks, 2 * kz * M, side).astype(BF16)),
+    )
+
+
+def ahead_x(pencil, mat):
+    bricks, pair, _, wins, modes, chans, lanes = pencil.shape
+    side, cols = mat.shape[1:]
+    return pl.pallas_call(
+        lambda *r: ahead_kernel(pair, wins, *r),
+        grid=(bricks,),
+        in_specs=[
+            pl.BlockSpec((1,) + pencil.shape[1:], lambda i: (i, 0, 0, 0, 0, 0, 0)),
+            pl.BlockSpec((1, side, cols), lambda i: (i, 0, 0)),
+        ],
+        out_specs=pl.BlockSpec((2, modes, pair * chans, cols // 2), lambda i: (0, 0, 0, 0)),
+        out_shape=jax.ShapeDtypeStruct((2, modes, pair * chans, cols // 2), F32),
+        scratch_shapes=[pltpu.VMEM((pair * modes * chans, cols), F32)],
+        compiler_params=params(),
+    )(pencil, mat)
+
+
+def back_kernel(pair, real_ref, imag_ref, mat_ref, out_ref):
+    modes, outs, lanes = real_ref.shape
+    chans = outs // pair
+    left = jnp.concatenate(
+        [real_ref[...].reshape(modes * outs, lanes), imag_ref[...].reshape(modes * outs, lanes)], axis=1
+    ).astype(BF16)
+    res = mm(left, mat_ref[0])
+    half = res.shape[1] // 2
+    res = res.reshape(modes, pair, chans, 2 * half)
+    for dest in range(pair):
+        for s in range(2):
+            piece = res[:, dest, :, s * half : (s + 1) * half]
+            out_ref[0, dest, s] = piece.reshape(modes * chans, half).astype(BF16)
+
+
+def back_x(real, imag, mat, pair):
+    bricks, rows, side = mat.shape
+    modes, outs, lanes = real.shape
+    shape = (bricks, pair, 2, modes * outs // pair, side // 2)
+    return pl.pallas_call(
+        lambda *r: back_kernel(pair, *r),
+        grid=(bricks,),
+        in_specs=[
+            pl.BlockSpec(real.shape, lambda i: (0, 0, 0)),
+            pl.BlockSpec(real.shape, lambda i: (0, 0, 0)),
+            pl.BlockSpec((1, rows, side), lambda i: (i, 0, 0)),
+        ],
+        out_specs=pl.BlockSpec((1,) + shape[1:], lambda i: (i, 0, 0, 0, 0)),
+        out_shape=jax.ShapeDtypeStruct(shape, BF16),
+        compiler_params=params(),
+    )(real, imag, mat)
+
+
+def inverse_kernel(pair, width, wins, span_ref, cell_ref, skip_ref, bias_ref, r_ref, ytab_ref, ztab_ref, out_ref, mat_ref, acc_ref):
     step = pl.program_id(0)
     first, last = span_ref[0, step], span_ref[1, step]
     planes = width * wins
+    kz = M // pair
+    rows = r_ref.shape[2]
+    lanes = width * kz
+    chans = out_ref.shape[0]
+
+    @pl.when(step == 0)
+    def _():
+        for win in range(wins):
+            for src in range(r_ref.shape[0] // pair):
+                parts = [
+                    r_ref[src * pair + half, s, :, win * lanes : (win + 1) * lanes]
+                    for s in range(2)
+                    for half in range(pair)
+                ]
+                mat_ref[win, src * rows : (src + 1) * rows, :] = jnp.concatenate(parts, axis=1)
 
     @pl.when(first >= planes)
     def _():
@@ -219,22 +336,34 @@
         count = cells.shape[1]
         x = cells >> 14
         acc_ref[...] = jnp.zeros_like(acc_ref)
-        zs = mm(ztab_ref[...], hot(cells & 127, G))
+        zs = -mm(ztab_ref[...], hot(cells & 127, G))
         for win in range(wins):
             @pl.when((first < (win + 1) * width) & (last >= win * width))
             def _():
-                pieces = [jnp.where(x == win * width + off, zs, 0.0) for off in range(width)]
-                right = jnp.concatenate(pieces, axis=0).astype(BF16)
-                acc_ref[...] += mm(r_ref[win], right)
+                masks = [x == win * width + off for off in range(width)]
+                sides = []
+                for s in range(2):
+                    pieces = []
+                    for half in range(pair):
+                        at = s * M + half * kz
+                        pieces += [jnp.where(mask, zs[at : at + kz], 0.0) for mask in masks]
+                    sides.append(jnp.concatenate(pieces, axis=0).astype(BF16))
+                mat = mat_ref[win]
+                acc_ref[0] += mm(mat, jnp.concatenate([-sides[0], sides[1]], axis=0))
+                acc_ref[1] += mm(mat, jnp.concatenate([sides[1], sides[0]], axis=0))
         ys = y_phases(ytab_ref, (cells >> 7) & 127)
-        field = jnp.sum(acc_ref[...].reshape(chans, 2 * M, count) * ys[None], axis=1)
+        field = jnp.zeros((chans, count), F32)
+        for s in range(2):
+            for b in range(M):
+                at = s * M + b
+                field += acc_ref[s, b * chans : (b + 1) * chans, :] * ys[at : at + 1]
         v = field * (1.0 / (G * math.sqrt(G))) + skip_ref[...] + bias_ref[...]
         out_ref[...] = jax.nn.gelu(v, approximate=True).astype(BF16)
 
 
-def inverse(cells, skip, bias, mat, span, planes, step):
+def inverse(cells, skip, bias, lines, span, planes, pair, step):
     chans, total = skip.shape
-    width = min(4, planes)
+    width = min(8, planes)
     wins = planes // width
     y_cos, y_sin = angles(M, True)
     z_cos, z_sin = angles(M, False)
@@ -245,7 +374,7 @@
     factor = np.where(np.arange(M) == 0, 1.0, 2.0)[:, None]
     ztab = jnp.asarray(np.concatenate([z_cos * factor, z_sin * factor]).astype(BF16))
     return pl.pallas_call(
-        lambda *r: inverse_kernel(chans, width, wins, *r),
+        lambda *r: inverse_kernel(pair, width, wins, *r),
         grid_spec=pltpu.PrefetchScalarGridSpec(
             num_scalar_prefetch=1,
             grid=(total // step,),
@@ -253,16 +382,19 @@
                 pl.BlockSpec((1, step), lambda i, s: (0, i)),
                 pl.BlockSpec((chans, step), lambda i, s: (0, i)),
                 pl.BlockSpec((chans, 1), lambda i, s: (0, 0)),
-                pl.BlockSpec(mat.shape, lambda i, s: (0, 0, 0)),
+                pl.BlockSpec(lines.shape, lambda i, s: (0, 0, 0, 0)),
                 pl.BlockSpec((4 * M, G), lambda i, s: (0, 0)),
                 pl.BlockSpec((2 * M, G), lambda i, s: (0, 0)),
             ],
             out_specs=pl.BlockSpec((chans, step), lambda i, s: (0, i)),
-            scratch_shapes=[pltpu.VMEM((chans * 2 * M, step), F32)],
+            scratch_shapes=[
+                pltpu.VMEM((wins, M * chans, 2 * width * M), BF16),
+                pltpu.VMEM((2, M * chans, step), F32),
+            ],
         ),
         out_shape=jax.ShapeDtypeStruct((chans, total), BF16),
         compiler_params=params(),
-    )(span, cells, skip, bias[:, None], mat, ytab, ztab)
+    )(span, cells, skip, bias[:, None], lines, ytab, ztab)
 
 
 def decode_kernel(chans, high, hid_ref, coef_ref, points_ref, out_ref):
@@ -352,38 +484,19 @@
     sent = spec.reshape(2, wins, chans, bricks, modes, pair, width * kz)
     sent = sent.transpose(3, 5, 0, 1, 4, 2, 6).reshape(bricks * pair, 2, wins, modes, chans, width * kz)
     pencil = lax.all_to_all(sent, both, split_axis=0, concat_axis=0, tiled=True)
-    pencil = pencil.reshape(bricks, pair, 2, wins, modes, chans, width, kz)
-    pencil = pencil.transpose(4, 1, 5, 7, 2, 0, 3, 6).reshape(modes, C, kz, 2 * G)
-
-    scale = 1.0 / (G * math.sqrt(G))
-    x_cos, x_sin = angles(M, True)
-    x_cos, x_sin = x_cos.T, x_sin.T
-    ahead = np.stack([np.concatenate([x_cos, x_sin]), np.concatenate([-x_sin, x_cos])])
-    ahead = jnp.asarray(ahead.astype(BF16))
-    coeff = jnp.einsum("bikx,rxa->rbika", pencil, ahead, preferred_element_type=F32) * scale
-    coeff = coeff.reshape(2, modes, C, kz * M)
+    pencil = pencil.reshape(bricks, pair, 2, wins, modes, chans, width * kz)
+    ahead, back = x_matrices(bricks, kz)
+    coeff = ahead_x(pencil, ahead)
     c_real, c_imag = coeff[0], coeff[1]
     w_real, w_imag = spectral_weight[0], spectral_weight[1]
     m_real = jnp.sum(w_real * c_real[:, :, None] - w_imag * c_imag[:, :, None], axis=1)
     m_imag = jnp.sum(w_real * c_imag[:, :, None] + w_imag * c_real[:, :, None], axis=1)
-    mixed = jnp.stack([m_real, m_imag]).astype(BF16).reshape(2, modes, C, kz, M)
-    back = np.stack([np.stack([x_cos, -x_sin]), np.stack([x_sin, x_cos])])
-    back = jnp.asarray(back.astype(BF16))
-    lines = jnp.einsum("sboka,rsxa->rbokx", mixed, back, preferred_element_type=F32).astype(BF16)
-    lines = lines.reshape(2, modes, pair, chans, kz, bricks, planes)
-    lines = lines.transpose(5, 2, 0, 1, 3, 4, 6).reshape(bricks * pair, 2, modes, chans, kz * planes)
+    lines = back_x(m_real, m_imag, back, pair)
+    lines = lines.reshape((bricks * pair,) + lines.shape[2:])
     lines = lax.all_to_all(lines, both, split_axis=0, concat_axis=0, tiled=True)
-    lines = lines.reshape(bricks, pair, 2, modes, chans, kz, planes)
-    wide = min(4, planes)
-    lines = lines.reshape(bricks, pair, 2, modes, chans, kz, planes // wide, wide)
-    lines = lines.transpose(2, 6, 4, 0, 3, 7, 1, 5).reshape(2, planes // wide, chans, M, wide, M)
-    r_real, r_imag = lines[0], lines[1]
-    top = jnp.stack([r_real, -r_imag], axis=4)
-    low = jnp.stack([-r_imag, -r_real], axis=4)
-    mat = jnp.stack([top, low], axis=2).reshape(planes // wide, chans * 2 * M, wide * 2 * M)
-
-    skip = skip_at(every, coef, cells, skip_weight, bricks, slots, slab_cells)
-    hidden = inverse(cells, skip, bias, mat, span, planes, step)
+
+    skip = skip_at(every, coef, cells, skip_weight, slab_cells)
+    hidden = inverse(cells, skip, bias, lines, span, planes, pair, step)
     answered = lax.all_to_all(
         hidden.reshape(chans, bricks, slots), "brick", split_axis=1, concat_axis=1, tiled=True
     )

time: 546 us -> 411 us (0.75)
  local copies, waits for them, and re-layouts: 186 us -> 30.2 us
  blocking collectives: 0 us -> 39.1 us
  Pallas kernels: 183 us -> 217 us
  starting transfers between devices: 70.9 us -> 46.1 us
  other arithmetic: 40.6 us -> 20 us
  waiting for transfers between devices: 45.1 us -> 34.1 us
    reshape x8 -> x0, local copies, waits for them, and re-layouts: 73.9 us -> none  [the longest x1 21.3 us: shards(): jnp.stack([top, low], axis=2)]
    all_to_all x0 -> x1, blocking collectives: none -> 39.1 us  [shards(): pencil = lax.all_to_all(sent, both, split_axis=0, concat_axis=0, tiled=True)]
    pallas_call x2 -> x4, Pallas kernels: 133 us -> 164 us  [the longest x1 101 us: skip_at(): pl.pallas_call(lambda *r: skip_kernel(chans, group, *r), grid_spec=pltpu....]
    transpose x1, local copies, waits for them, and re-layouts: 26.2 us -> 0.68 us  [shards(): sent.transpose(3, 5, 0, 1, 4, 2, 6)]
    neg x2 -> x0, local copies, waits for them, and re-layouts: 21.5 us -> none  [shards(): top = jnp.stack([r_real, -r_imag], axis=4)]
    all_to_all x1 -> x0, starting transfers between devices: 17.7 us -> none  [shards(): pencil = lax.all_to_all(sent, both, split_axis=0, concat_axis=0, tiled=True)]
    another operation x5 -> x2, local copies, waits for them, and re-layouts: 23.8 us -> 6.27 us  [the longest x1 16.4 us: shards(): jnp.stack([top, low], axis=2)]
    all_to_all x1 -> x0, waiting for transfers between devices: 16.9 us -> none  [shards(): pencil = lax.all_to_all(sent, both, split_axis=0, concat_axis=0, tiled=True)]
  transfers between devices with their start and end apart: 6 -> 5, of which waited for: 3 -> 3; matrix products, arithmetic and copies ran while one was open for 18% -> 6% of each run, Pallas kernels for 18% -> 27%
where the time goes in v2:
time: 411 us; the launch traced here: 403 us
  Pallas kernels  217 us (53%)
  starting transfers between devices  46.1 us (11%)
  blocking collectives  39.1 us (10%)
  waiting for transfers between devices  34.1 us (8%)
  local copies, waits for them, and re-layouts  30.2 us (7%)
  other arithmetic  20 us (5%)
  between operations  13.3 us (3%)
    pallas_call x1, Pallas kernels, skip_at(): pl.pallas_call(lambda *r: skip_kernel(chans, group, *r), grid_spec=pltpu....  101 us
    pallas_call x1, Pallas kernels, inverse(): pl.pallas_call(lambda *r: inverse_kernel(pair, width, wins, *r), grid_spe...  48.2 us
    pallas_call x1, Pallas kernels, forward(): pl.pallas_call(lambda *r: forward_kernel(chans, width, wins, *r), grid_sp...  39.2 us
    all_to_all x1, blocking collectives, shards(): pencil = lax.all_to_all(sent, both, split_axis=0, concat_axis=0, tiled=True)  39.1 us
    all_to_all x1, starting transfers between devices, shards(): lax.all_to_all(hidden.reshape(chans, bricks, slots), 'brick', split_axis=...  27.9 us
    all_to_all x1, waiting for transfers between devices, shards(): lax.all_to_all(hidden.reshape(chans, bricks, slots), 'brick', split_axis=...  14.9 us
    all_to_all x1, waiting for transfers between devices, shards(): lax.all_to_all(picked.reshape(chans, bricks, slots), 'brick', split_axis=...  13.5 us
  transfers between devices with their start and end apart: 5, of which 3 were waited for; matrix products, arithmetic and copies ran while one was open for 6% of the time, Pallas kernels for 27%

profile of v2, /device:TPU:0, one launch (start us, length us, event | category | flops | bytes accessed | tf_op | source)
XLA Modules:
  0.0 402.8 jit_solution(15842989320755451488)
XLA Ops:
  6.5 1.6 bitcast_select_fusion.2
  8.1 1.6 bitcast_select_fusion
  9.7 7.9 %sort.37.cloned.1.call-done = (s32[8,2048]{1,0:T(8,128)}, s32[8,2048]{1,0:T(8,128)}, f32[8,2048]{1,0:T(8,128)}, f32[8,2048]{1,0:T(8,128)}) async-done(((s32[8,2048]{1,0:T(8,128)}, s32[8,2048]{1,0:T(8,128)}, f32[8,2048]{1,0:T(8,128)}, f32[8,2048]{1,0:T(8,128)}), (s32[8,2048]{1,0:T(8,128)}, s32[8,2048]{1,0:T(8,128)}, f32[8,2048]{1,0:T(8,128)}, f32[8,2048]{1,0:T(8,128)})) %sort.37.cloned.1.call-update) | async-done | bytes 262160 | tf_op jit(solution)/shard_map/sort | solution.py:461
  17.6 0.8 convert_element_type.40
  18.5 0.9 stack.13
  19.4 0.8 pad_maximum_fusion.1
  20.2 7.1 %all-to-all-start = ((f32[8,2,2048]{2,1,0:T(2,128)}), f32[8,2,2048]{2,1,0:T(2,128)S(1)}, u32[]{:S(2)}, u32[]{:S(2)}) async-start(f32[8,2,2048]{2,1,0:T(2,128)} %pad_maximum_fusion.1), calls=%async_computation | async-start | bytes 262144 | tf_op jit(solution)/shard_map/all_to_all | solution.py:468
  27.3 0.9 reshape.80.r_0_
  28.1 0.9 copy.53
  29.1 6.0 %shard_map.145 = bf16[16,16384]{1,0:T(8,128)(2,1)S(1)} custom-call(bf16[256,128]{1,0:T(8,128)(2,1)S(1)} %reshape.80.r_0_, s32[1,16384]{1,0:T(1,128)S(1)} %bitcast.78), custom_call_target="tpu_custom_call" | custom-call | tf_op jit(solution)/shard_map/pallas_call | solution.py:54
  35.1 0.8 copy.58
  35.9 6.0 %all-to-all-start.1 = ((bf16[16,8,2048]{2,0,1:T(8,128)(2,1)}), bf16[16,8,2048]{2,0,1:T(8,128)(2,1)S(1)}, u32[]{:S(2)}, u32[]{:S(2)}) async-start(bf16[16,8,2048]{2,0,1:T(8,128)(2,1)} %bitcast.65), calls=%async_computation.1 | async-start | bytes 1048576 | tf_op jit(solution)/shard_map/all_to_all | solution.py:471
  42.0 0.2 shift-right-arithmetic_reduce_fusion
  42.2 0.2 slice_reduce_fusion.3
  42.4 0.1 fusion.9
  42.5 13.5 %all-to-all-done.1 = bf16[16,8,2048]{2,0,1:T(8,128)(2,1)S(1)} async-done(((bf16[16,8,2048]{2,0,1:T(8,128)(2,1)}), bf16[16,8,2048]{2,0,1:T(8,128)(2,1)S(1)}, u32[]{:S(2)}, u32[]{:S(2)}) %all-to-all-start.1) | async-done | bytes 524320 | tf_op jit(solution)/shard_map/all_to_all | solution.py:471
  56.0 0.8 copy-done.3
  56.8 0.7 copy-done.7
  57.5 39.2 %shard_map.147 = bf16[2,2,16,32,256]{4,3,2,1,0:T(8,128)(2,1)S(1)} custom-call(s32[2,64]{1,0:T(2,128)S(1)} %pad_add_fusion.r_0_, bf16[16,16384]{1,0:T(8,128)(2,1)S(1)} %bitcast.66, f32[1,16384]{1,0:T(1,128)S(1)} %bitcast.80, s32[1,16384]{1,0:T(1,128)S(1)} %bitcast.68, bf16[128,128]{1,0:T(8,128)(2,1)S(1)} %copy-done.3, bf16[64,128]{1,0:T(8,128)(2,1)S(1)} %copy-done.7), custom_call_target="tpu_custom_call" | custom-call | tf_op jit(solution)/shard_map/pallas_call | solution.py:123
  96.7 0.3 reshape.84
  97.0 0.7 copy.45
  97.7 39.1 %all_to_all.25 = bf16[16,2,2,4,16,128]{5,4,3,2,1,0:T(8,128)(2,1)S(1)} all-to-all(bf16[16,2,2,4,16,128]{5,4,3,2,1,0:T(8,128)(2,1)S(1)} %bitcast.87), channel_id=1, replica_groups=mesh['groups'=2,'brick'=8,'chan'=2] {'brick','chan'}, dimensions={0} | all-to-all | bytes 2097152 | tf_op jit(solution)/shard_map/all_to_all | solution.py:486
  136.8 7.0 %shard_map.148 = f32[2,4,32,512]{3,2,1,0:T(8,128)S(1)} custom-call(bf16[8,2,2,2,4,16,128]{6,5,4,3,2,1,0:T(8,128)(2,1)S(1)} %bitcast.74, bf16[8,512,1024]{2,1,0:T(8,128)(2,1)} %constant.25.clone.r_1_), custom_call_target="tpu_custom_call" | custom-call | tf_op jit(solution)/shard_map/pallas_call | solution.py:262
  143.9 7.9 %fusion.3 = (f32[4,32,512]{2,1,0:T(8,128)S(1)}, f32[4,32,512]{2,1,0:T(8,128)S(1)}) fusion(f32[2,4,32,32,512]{4,3,2,1,0:T(8,128)} %param.22, f32[4,32,512]{2,1,0:T(8,128)S(1)} %get-tuple-element.23, f32[4,32,512]{2,1,0:T(8,128)S(1)} %get-tuple-element.22), kind=kLoop, calls=%fused_computation.5 | loop fusion | flops 16646144 | bytes 17825792 | tf_op jit(solution)/shard_map/reduce_sum | solution.py:493
  151.9 7.8 %shard_map.149 = bf16[8,2,2,64,256]{4,3,2,1,0:T(8,128)(2,1)} custom-call(f32[4,32,512]{2,1,0:T(8,128)S(1)} %get-tuple-element.14.r_0_, f32[4,32,512]{2,1,0:T(8,128)S(1)} %get-tuple-element.13.r_1_, bf16[8,1024,512]{2,1,0:T(8,128)(2,1)} %constant.26.clone.r_2_), custom_call_target="tpu_custom_call" | custom-call | tf_op jit(solution)/shard_map/pallas_call | solution.py:295
  159.7 5.0 %all-to-all-start.3 = ((bf16[16,2,64,256]{3,2,1,0:T(8,128)(2,1)}), bf16[16,2,64,256]{3,2,1,0:T(8,128)(2,1)S(1)}, u32[]{:S(2)}, u32[]{:S(2)}) async-start(bf16[16,2,64,256]{3,2,1,0:T(8,128)(2,1)} %bitcast.21), calls=%async_computation.3 | async-start | bytes 2097152 | tf_op jit(solution)/shard_map/all_to_all | solution.py:496
  164.7 0.0 all-gather.2.cloned.1.call-start
  164.7 0.7 all-gather.2.cloned.1.call-update
  165.5 0.1 copy.46.r_3_
  165.6 4.9 %copy.44.r_2_ = s32[16384,1]{1,0:T(8,128)} copy(s32[16384,1]{0,1:T(1,128)S(1)} %bitcast.69) | data formatting | bytes 131072 | tf_op jit(solution)/shard_map/convert_element_type | solution.py:469
  170.4 0.1 compare_reduce_fusion
  170.6 0.2 minimum_reduce_fusion
  170.8 0.8 iota_select_fusion
  171.6 5.1 %all-gather.2.cloned.1.call-done = bf16[32,16384]{1,0:T(8,128)(2,1)} async-done(((bf16[16,16384]{1,0:T(8,128)(2,1)}), bf16[32,16384]{1,0:T(8,128)(2,1)}) %all-gather.2.cloned.1.call-update) | async-done | bytes 1048592 | tf_op jit(solution)/shard_map/all_gather | solution.py:474
  176.7 2.6 reduce-precision_convert_fusion
  179.3 3.1 copy.42
  182.4 3.1 copy.43
  185.5 6.0 %pad_maximum_fusion.r_4_ = bf16[128,128,32]{2,1,0:T(8,128)(2,1)} fusion(bf16[128,128,16]{2,1,0:T(8,128)(2,1)} %bitcast.85, bf16[128,128,16]{2,1,0:T(8,128)(2,1)} %bitcast.84), kind=kLoop, calls=%fused_computation.8 | loop fusion | flops 2097152 | bytes 2097152 | tf_op jit(solution)/shard_map/concatenate | solution.py:182
  191.5 2.2 copy-done.1
  193.7 0.8 copy-done.5
  194.5 101.1 %shard_map.146.r_2_ = f32[16,16384]{1,0:T(8,128)S(1)} custom-call(s32[128]{0:T(128)S(1)} %get-tuple-element.27.r_0_, s32[128,1,128]{2,1,0:T(1,128)S(1)} %bitcast.83, s32[16384,1]{1,0:T(8,128)} %copy.44.r_2_, s32[128,128]{1,0:T(8,128)S(1)} %bitcast.72, bf16[128,128,32]{2,1,0:T(8,128)(2,1)S(1)} %copy-done.1), custom_call_target="tpu_custom_call" | custom-call | tf_op jit(solution)/shard_map/pallas_call | solution.py:192
  295.7 48.2 %shard_map.150 = bf16[16,16384]{1,0:T(8,128)(2,1)S(1)} custom-call(s32[2,64]{1,0:T(2,128)S(1)} %pad_add_fusion.r_0_, s32[1,16384]{1,0:T(1,128)S(1)} %bitcast.73, f32[16,16384]{1,0:T(8,128)S(1)} %shard_map.146.r_2_, f32[16,1]{1,0:T(8,128)S(1)} %copy.46.r_3_, bf16[16,2,64,256]{3,2,1,0:T(8,128)(2,1)S(1)} %all-to-all-done.3.r_4_, ...), custom_call_target="tpu_custom_call" | custom-call | tf_op jit(solution)/shard_map/pallas_call | solution.py:376
  344.0 0.8 copy.57
  344.8 27.9 %all-to-all-start.4 = ((bf16[16,8,2048]{2,0,1:T(8,128)(2,1)}), bf16[16,8,2048]{2,0,1:T(8,128)(2,1)S(1)}, u32[]{:S(2)}, u32[]{:S(2)}) async-start(bf16[16,8,2048]{2,0,1:T(8,128)(2,1)} %bitcast.64), calls=%async_computation.4 | async-start | bytes 1048576 | tf_op jit(solution)/shard_map/all_to_all | solution.py:500
  372.7 0.1 copy.54
  372.8 14.9 %all-to-all-done.4 = bf16[16,8,2048]{2,0,1:T(8,128)(2,1)S(1)} async-done(((bf16[16,8,2048]{2,0,1:T(8,128)(2,1)}), bf16[16,8,2048]{2,0,1:T(8,128)(2,1)S(1)}, u32[]{:S(2)}, u32[]{:S(2)}) %all-to-all-start.4) | async-done | bytes 524320 | tf_op jit(solution)/shard_map/all_to_all | solution.py:500
  387.7 7.9 %shard_map.151 = f32[256,128]{1,0:T(8,128)S(1)} custom-call(bf16[16,16384]{1,0:T(8,128)(2,1)S(1)} %bitcast.77, f32[1,16384]{1,0:T(1,128)S(1)} %bitcast.82, s32[1,16384]{1,0:T(1,128)S(1)} %bitcast.79), custom_call_target="tpu_custom_call" | custom-call | tf_op jit(solution)/shard_map/pallas_call | solution.py:422
  395.6 0.7 reshape.91
  (29 shorter events, 0.3 us)
Async XLA Ops:
  6.5 170.1 %copy-start = (f32[16,32]{1,0:T(8,128)S(1)}, f32[16,32]{1,0:T(8,128)}, u32[]{:S(2)}) copy-start(f32[16,32]{1,0:T(8,128)} %param.21) | copy-start | bytes 6148
  6.5 11.1 %sort.37.cloned.1.call-start = ((), (), s32[]{:S(2)}) async-start(), calls=%async_computation.6 | async-start | bytes 786464 | tf_op jit(solution)/shard_map/sort | solution.py:461
  20.2 15.8 %all-to-all-start = ((f32[8,2,2048]{2,1,0:T(2,128)}), f32[8,2,2048]{2,1,0:T(2,128)S(1)}, u32[]{:S(2)}, u32[]{:S(2)}) async-start(f32[8,2,2048]{2,1,0:T(2,128)} %pad_maximum_fusion.1), calls=%async_computation | async-start | bytes 262144 | tf_op jit(solution)/shard_map/all_to_all | solution.py:468
  35.9 20.0 %all-to-all-start.1 = ((bf16[16,8,2048]{2,0,1:T(8,128)(2,1)}), bf16[16,8,2048]{2,0,1:T(8,128)(2,1)S(1)}, u32[]{:S(2)}, u32[]{:S(2)}) async-start(bf16[16,8,2048]{2,0,1:T(8,128)(2,1)} %bitcast.65), calls=%async_computation.1 | async-start | bytes 1048576 | tf_op jit(solution)/shard_map/all_to_all | solution.py:471
  56.0 87.9 %copy-start.2 = (bf16[8,2,8,2048]{3,2,0,1:T(8,128)(2,1)}, bf16[8,2,8,2048]{3,2,0,1:T(8,128)(2,1)S(1)}, u32[]{:S(2)}) copy-start(bf16[8,2,8,2048]{3,2,0,1:T(8,128)(2,1)S(1)} %copy.51) | copy-start | bytes 1572868
  56.0 0.8 copy-start.3
  56.8 0.7 copy-start.7
  151.8 13.6 %copy-start.9 = (f32[16]{0:T(128)S(1)}, f32[16]{0:T(128)}, u32[]{:S(2)}) copy-start(f32[16]{0:T(128)} %param.23) | copy-start | bytes 196
  159.7 136.0 %all-to-all-start.3 = ((bf16[16,2,64,256]{3,2,1,0:T(8,128)(2,1)}), bf16[16,2,64,256]{3,2,1,0:T(8,128)(2,1)S(1)}, u32[]{:S(2)}, u32[]{:S(2)}) async-start(bf16[16,2,64,256]{3,2,1,0:T(8,128)(2,1)} %bitcast.21), calls=%async_computation.3 | async-start | bytes 2097152 | tf_op jit(solution)/shard_map/all_to_all | solution.py:496
  164.7 12.0 %all-gather.2.cloned.1.call-start = ((), (), s32[]{:S(2)}) async-start(), calls=%async_computation.5 | async-start | bytes 1572864 | tf_op jit(solution)/shard_map/all_gather | solution.py:474
  165.4 26.1 %sort.39.cloned.1.call-start = ((), (), s32[]{:S(2)}) async-start(), calls=%async_computation.7 | async-start | bytes 196640 | tf_op jit(solution)/shard_map/sort | solution.py:190
  185.5 110.2 %copy-start.4 = (bf16[128,128]{1,0:T(8,128)(2,1)S(1)}, bf16[128,128]{1,0:T(8,128)(2,1)}, u32[]{:S(2)}) copy-start(bf16[128,128]{1,0:T(8,128)(2,1)} %constant.10.clone.r_4_.r_5_) | copy-start | bytes 98308
  185.5 110.2 %copy-start.6 = (bf16[64,128]{1,0:T(8,128)(2,1)S(1)}, bf16[64,128]{1,0:T(8,128)(2,1)}, u32[]{:S(2)}) copy-start(bf16[64,128]{1,0:T(8,128)(2,1)} %constant.27.clone.r_6_) | copy-start | bytes 49156
  191.5 2.2 copy-start.1
  193.7 0.8 copy-start.5
  194.5 178.2 %copy-start.8 = (f32[8,2048]{1,0:T(8,128)S(1)}, f32[8,2048]{1,0:T(8,128)}, u32[]{:S(2)}) copy-start(f32[8,2048]{1,0:T(8,128)} %get-tuple-element.12) | copy-start | bytes 196612
  344.8 42.9 %all-to-all-start.4 = ((bf16[16,8,2048]{2,0,1:T(8,128)(2,1)}), bf16[16,8,2048]{2,0,1:T(8,128)(2,1)S(1)}, u32[]{:S(2)}, u32[]{:S(2)}) async-start(bf16[16,8,2048]{2,0,1:T(8,128)(2,1)} %bitcast.64), calls=%async_computation.4 | async-start | bytes 1048576 | tf_op jit(solution)/shard_map/all_to_all | solution.py:500
Sparse Core Ops, SparseCore 0:
  9.9 7.3 sort.41.cloned.1.call-done
  167.1 9.4 all-gather.1
  179.0 5.7 sort.43.cloned.1.call-done
  (2 shorter events, 0.0 us)

commit v3 on v2

--- a/solution.py
+++ b/solution.py
@@ -140,34 +140,36 @@
     )(span, feats, coef, cells, ytab, ztab)
 
 
-def skip_kernel(chans, group, count_ref, work_ref, mine_ref, cells_ref, vals_ref, out_ref):
-    live = count_ref[pl.program_id(0)]
-    mine = mine_ref[...]
-
-    def one(turn, acc):
-        hits = []
-        vals = []
-        for off in range(group):
-            at = turn * group + off
-            row = work_ref[0, 0, at]
-            other = jnp.where(at < live, cells_ref[pl.ds(row, 1), :], -1)
-            hits.append(jnp.where(mine == other, 1.0, 0.0).astype(BF16))
-            vals.append(vals_ref[row])
-        hit = jnp.concatenate(hits, axis=1)
-        val = jnp.concatenate(vals, axis=0)
-        return acc + mm(hit, val)
-
-    rounds = (live + group - 1) // group
-    acc = lax.fori_loop(0, rounds, one, jnp.zeros((128, 2 * chans), F32))
+def skip_kernel(chans, group, batch, count_ref, work_ref, cells_ref, vals_ref, out_ref):
     rows = lax.broadcasted_iota(jnp.int32, (chans, 2 * chans), 0)
     cols = lax.broadcasted_iota(jnp.int32, (chans, 2 * chans), 1)
     fold = jnp.where((cols == rows) | (cols == rows + chans), 1.0, 0.0)
-    out_ref[...] = lax.dot_general(
-        fold, acc, NT, precision=lax.Precision.HIGHEST, preferred_element_type=F32
-    )
-
-
-def skip_at(feats, coef, cells, weight, slab_cells, group=8):
+    for part in range(batch):
+        chunk = pl.program_id(0) * batch + part
+        live = count_ref[chunk]
+        mine = jnp.transpose(jnp.broadcast_to(cells_ref[pl.ds(chunk, 1), :], (128, 128)))
+
+        def one(turn, acc):
+            hits = []
+            vals = []
+            for off in range(group):
+                at = turn * group + off
+                row = work_ref[part, 0, at]
+                other = jnp.where(at < live, cells_ref[pl.ds(row, 1), :], -1)
+                hits.append(jnp.where(mine == other, 1.0, 0.0).astype(BF16))
+                vals.append(vals_ref[row])
+            hit = jnp.concatenate(hits, axis=1)
+            val = jnp.concatenate(vals, axis=0)
+            return acc + mm(hit, val)
+
+        rounds = (live + group - 1) // group
+        acc = lax.fori_loop(0, rounds, one, jnp.zeros((128, 2 * chans), F32))
+        out_ref[:, part * 128 : (part + 1) * 128] = lax.dot_general(
+            fold, acc, NT, precision=lax.Precision.HIGHEST, preferred_element_type=F32
+        )
+
+
+def skip_at(feats, coef, cells, weight, slab_cells, group=8, batch=8):
     chans = weight.shape[0]
     total = cells.shape[1]
     chunks = total // 128
@@ -190,21 +192,20 @@
     work = lax.sort(jnp.where(meets, places[None], chunks - 1), dimension=1)
     count = jnp.sum(meets.astype(jnp.int32), axis=1)
     return pl.pallas_call(
-        lambda *r: skip_kernel(chans, group, *r),
+        lambda *r: skip_kernel(chans, group, batch, *r),
         grid_spec=pltpu.PrefetchScalarGridSpec(
             num_scalar_prefetch=1,
-            grid=(chunks,),
+            grid=(chunks // batch,),
             in_specs=[
-                pl.BlockSpec((1, 1, chunks), lambda i, a: (i, 0, 0), memory_space=pltpu.SMEM),
-                pl.BlockSpec((128, 1), lambda i, a: (i, 0)),
+                pl.BlockSpec((batch, 1, chunks), lambda i, a: (i, 0, 0), memory_space=pltpu.SMEM),
                 pl.BlockSpec((chunks, 128), lambda i, a: (0, 0)),
                 pl.BlockSpec((chunks, 128, 2 * chans), lambda i, a: (0, 0, 0)),
             ],
-            out_specs=pl.BlockSpec((chans, 128), lambda i, a: (0, i)),
+            out_specs=pl.BlockSpec((chans, batch * 128), lambda i, a: (0, i)),
         ),
         out_shape=jax.ShapeDtypeStruct((chans, total), F32),
         compiler_params=params(),
-    )(count, work.reshape(chunks, 1, chunks), cells.reshape(total, 1), rows, both)
+    )(count, work.reshape(chunks, 1, chunks), rows, both)
 
 
 def ahead_kernel(pair, wins, in_ref, mat_ref, out_ref, acc_ref):

time: 411 us -> 386 us (0.939); the launches traced: 403 us -> 386 us
  Pallas kernels: 217 us -> 158 us
  starting transfers between devices: 46.1 us -> 80.6 us
  blocking collectives: 39.1 us -> 48 us
  local copies, waits for them, and re-layouts: 30.2 us -> 25.2 us
  waiting for transfers between devices: 34.1 us -> 39 us
    pallas_call x1, Pallas kernels: 101 us -> 63.4 us  [skip_at(): pl.pallas_call(lambda *r: skip_kernel(chans, group, batch, *r), grid_spec...]
    all_to_all x1, starting transfers between devices: 27.9 us -> 62.3 us  [shards(): lax.all_to_all(hidden.reshape(chans, bricks, slots), 'brick', split_axis=...]
    pallas_call x1, Pallas kernels: 48.2 us -> 35.8 us  [inverse(): pl.pallas_call(lambda *r: inverse_kernel(pair, width, wins, *r), grid_spe...]
    pallas_call x1, Pallas kernels: 39.2 us -> 29.6 us  [forward(): pl.pallas_call(lambda *r: forward_kernel(chans, width, wins, *r), grid_sp...]
    all_to_all x1, blocking collectives: 39.1 us -> 48 us  [shards(): pencil = lax.all_to_all(sent, both, split_axis=0, concat_axis=0, tiled=True)]
    convert_element_type x1 -> x0, local copies, waits for them, and re-layouts: 4.86 us -> none  [shards(): cells = meta[:, 0].astype(jnp.int32).reshape(1, -1)]
    all_gather x1, waiting for transfers between devices: 5.11 us -> 9.97 us  [shards(): every = lax.all_gather(got, 'chan', axis=0, tiled=True)]
  transfers between devices with their start and end apart: 5 -> 5, of which waited for: 3 -> 3; matrix products, arithmetic and copies ran while one was open for 6% -> 5% of each run, Pallas kernels for 27% -> 18%
where the time goes in v3:
time: 386 us
  Pallas kernels  158 us (41%)
  starting transfers between devices  80.6 us (21%)
  blocking collectives  48 us (12%)
  waiting for transfers between devices  39 us (10%)
  local copies, waits for them, and re-layouts  25.2 us (7%)
  other arithmetic  20 us (5%)
  between operations  13.3 us (3%)
    pallas_call x1, Pallas kernels, skip_at(): pl.pallas_call(lambda *r: skip_kernel(chans, group, batch, *r), grid_spec...  63.4 us
    all_to_all x1, starting transfers between devices, shards(): lax.all_to_all(hidden.reshape(chans, bricks, slots), 'brick', split_axis=...  62.3 us
    all_to_all x1, blocking collectives, shards(): pencil = lax.all_to_all(sent, both, split_axis=0, concat_axis=0, tiled=True)  48 us
    pallas_call x1, Pallas kernels, inverse(): pl.pallas_call(lambda *r: inverse_kernel(pair, width, wins, *r), grid_spe...  35.8 us
    pallas_call x1, Pallas kernels, forward(): pl.pallas_call(lambda *r: forward_kernel(chans, width, wins, *r), grid_sp...  29.6 us
    all_to_all x1, waiting for transfers between devices, shards(): lax.all_to_all(hidden.reshape(chans, bricks, slots), 'brick', split_axis=...  14.9 us
    all_to_all x1, waiting for transfers between devices, shards(): lax.all_to_all(picked.reshape(chans, bricks, slots), 'brick', split_axis=...  13.5 us
    all_gather x1, waiting for transfers between devices, shards(): every = lax.all_gather(got, 'chan', axis=0, tiled=True)  9.97 us
  transfers between devices with their start and end apart: 5, of which 3 were waited for; matrix products, arithmetic and copies ran while one was open for 5% of the time, Pallas kernels for 18%

profile of v3, /device:TPU:0, one launch (start us, length us, event | category | flops | bytes accessed | tf_op | source)
XLA Modules:
  0.0 386.4 jit_solution(3563327014920498461)
XLA Ops:
  6.5 1.6 bitcast_select_fusion.2
  8.1 1.6 bitcast_select_fusion
  9.7 7.7 %sort.37.cloned.1.call-done = (s32[8,2048]{1,0:T(8,128)}, s32[8,2048]{1,0:T(8,128)}, f32[8,2048]{1,0:T(8,128)}, f32[8,2048]{1,0:T(8,128)}) async-done(((s32[8,2048]{1,0:T(8,128)}, s32[8,2048]{1,0:T(8,128)}, f32[8,2048]{1,0:T(8,128)}, f32[8,2048]{1,0:T(8,128)}), (s32[8,2048]{1,0:T(8,128)}, s32[8,2048]{1,0:T(8,128)}, f32[8,2048]{1,0:T(8,128)}, f32[8,2048]{1,0:T(8,128)})) %sort.37.cloned.1.call-update) | async-done | bytes 262160 | tf_op jit(solution)/shard_map/sort | solution.py:462
  17.4 0.9 stack.13
  18.3 0.8 convert_element_type.30
  19.2 0.8 pad_maximum_fusion.1
  20.0 7.3 %all-to-all-start = ((f32[8,2,2048]{2,1,0:T(2,128)}), f32[8,2,2048]{2,1,0:T(2,128)S(1)}, u32[]{:S(2)}, u32[]{:S(2)}) async-start(f32[8,2,2048]{2,1,0:T(2,128)} %pad_maximum_fusion.1), calls=%async_computation | async-start | bytes 262144 | tf_op jit(solution)/shard_map/all_to_all | solution.py:469
  27.3 0.9 reshape.69.r_0_
  28.2 0.9 copy.49
  29.1 6.0 %shard_map.145 = bf16[16,16384]{1,0:T(8,128)(2,1)S(1)} custom-call(bf16[256,128]{1,0:T(8,128)(2,1)S(1)} %reshape.69.r_0_, s32[1,16384]{1,0:T(1,128)S(1)} %bitcast.76), custom_call_target="tpu_custom_call" | custom-call | tf_op jit(solution)/shard_map/pallas_call | solution.py:54
  35.1 0.8 copy.54
  36.0 6.0 %all-to-all-start.1 = ((bf16[16,8,2048]{2,0,1:T(8,128)(2,1)}), bf16[16,8,2048]{2,0,1:T(8,128)(2,1)S(1)}, u32[]{:S(2)}, u32[]{:S(2)}) async-start(bf16[16,8,2048]{2,0,1:T(8,128)(2,1)} %bitcast.64), calls=%async_computation.1 | async-start | bytes 1048576 | tf_op jit(solution)/shard_map/all_to_all | solution.py:472
  42.0 0.2 shift-right-arithmetic_reduce_fusion
  42.2 0.2 slice_reduce_fusion.3
  42.4 0.1 fusion.9
  42.5 13.5 %all-to-all-done.1 = bf16[16,8,2048]{2,0,1:T(8,128)(2,1)S(1)} async-done(((bf16[16,8,2048]{2,0,1:T(8,128)(2,1)}), bf16[16,8,2048]{2,0,1:T(8,128)(2,1)S(1)}, u32[]{:S(2)}, u32[]{:S(2)}) %all-to-all-start.1) | async-done | bytes 524320 | tf_op jit(solution)/shard_map/all_to_all | solution.py:472
  56.1 0.8 copy-done.3
  56.8 0.7 copy-done.7
  57.6 29.6 %shard_map.147 = bf16[2,2,16,32,256]{4,3,2,1,0:T(8,128)(2,1)S(1)} custom-call(s32[2,64]{1,0:T(2,128)S(1)} %pad_add_fusion.r_0_, bf16[16,16384]{1,0:T(8,128)(2,1)S(1)} %bitcast.65, f32[1,16384]{1,0:T(1,128)S(1)} %bitcast.78, s32[1,16384]{1,0:T(1,128)S(1)} %bitcast.68, bf16[128,128]{1,0:T(8,128)(2,1)S(1)} %copy-done.3, bf16[64,128]{1,0:T(8,128)(2,1)S(1)} %copy-done.7), custom_call_target="tpu_custom_call" | custom-call | tf_op jit(solution)/shard_map/pallas_call | solution.py:123
  87.1 0.3 reshape.73
  87.4 0.7 copy.41
  88.1 48.0 %all_to_all.25 = bf16[16,2,2,4,16,128]{5,4,3,2,1,0:T(8,128)(2,1)S(1)} all-to-all(bf16[16,2,2,4,16,128]{5,4,3,2,1,0:T(8,128)(2,1)S(1)} %bitcast.85), channel_id=1, replica_groups=mesh['groups'=2,'brick'=8,'chan'=2] {'brick','chan'}, dimensions={0} | all-to-all | bytes 2097152 | tf_op jit(solution)/shard_map/all_to_all | solution.py:487
  136.1 7.0 %shard_map.148 = f32[2,4,32,512]{3,2,1,0:T(8,128)S(1)} custom-call(bf16[8,2,2,2,4,16,128]{6,5,4,3,2,1,0:T(8,128)(2,1)S(1)} %bitcast.67, bf16[8,512,1024]{2,1,0:T(8,128)(2,1)} %constant.25.clone.r_1_), custom_call_target="tpu_custom_call" | custom-call | tf_op jit(solution)/shard_map/pallas_call | solution.py:263
  143.2 7.9 %fusion.3 = (f32[4,32,512]{2,1,0:T(8,128)S(1)}, f32[4,32,512]{2,1,0:T(8,128)S(1)}) fusion(f32[2,4,32,32,512]{4,3,2,1,0:T(8,128)} %param.22, f32[4,32,512]{2,1,0:T(8,128)S(1)} %get-tuple-element.23, f32[4,32,512]{2,1,0:T(8,128)S(1)} %get-tuple-element.22), kind=kLoop, calls=%fused_computation.5 | loop fusion | flops 16646144 | bytes 17825792 | tf_op jit(solution)/shard_map/reduce_sum | solution.py:494
  151.1 7.8 %shard_map.149 = bf16[8,2,2,64,256]{4,3,2,1,0:T(8,128)(2,1)} custom-call(f32[4,32,512]{2,1,0:T(8,128)S(1)} %get-tuple-element.14.r_0_, f32[4,32,512]{2,1,0:T(8,128)S(1)} %get-tuple-element.13.r_1_, bf16[8,1024,512]{2,1,0:T(8,128)(2,1)} %constant.26.clone.r_2_), custom_call_target="tpu_custom_call" | custom-call | tf_op jit(solution)/shard_map/pallas_call | solution.py:296
  159.0 5.0 %all-to-all-start.3 = ((bf16[16,2,64,256]{3,2,1,0:T(8,128)(2,1)}), bf16[16,2,64,256]{3,2,1,0:T(8,128)(2,1)S(1)}, u32[]{:S(2)}, u32[]{:S(2)}) async-start(bf16[16,2,64,256]{3,2,1,0:T(8,128)(2,1)} %bitcast.20), calls=%async_computation.3 | async-start | bytes 2097152 | tf_op jit(solution)/shard_map/all_to_all | solution.py:497
  164.0 0.0 all-gather.2.cloned.1.call-start
  164.0 0.7 all-gather.2.cloned.1.call-update
  164.7 0.2 sort.39.cloned.1.call-start
  165.0 0.1 copy.42.r_3_
  165.1 0.1 compare_reduce_fusion
  165.2 0.2 minimum_reduce_fusion
  165.4 0.8 iota_select_fusion
  166.2 10.0 %all-gather.2.cloned.1.call-done = bf16[32,16384]{1,0:T(8,128)(2,1)} async-done(((bf16[16,16384]{1,0:T(8,128)(2,1)}), bf16[32,16384]{1,0:T(8,128)(2,1)}) %all-gather.2.cloned.1.call-update) | async-done | bytes 1048592 | tf_op jit(solution)/shard_map/all_gather | solution.py:475
  176.1 2.6 reduce-precision_convert_fusion
  178.7 3.1 copy.40
  181.8 3.1 copy.39
  184.9 6.0 %pad_maximum_fusion.r_3_ = bf16[128,128,32]{2,1,0:T(8,128)(2,1)} fusion(bf16[128,128,16]{2,1,0:T(8,128)(2,1)} %bitcast.82, bf16[128,128,16]{2,1,0:T(8,128)(2,1)} %bitcast.83), kind=kLoop, calls=%fused_computation.8 | loop fusion | flops 2097152 | bytes 2097152 | tf_op jit(solution)/shard_map/concatenate | solution.py:184
  190.9 2.2 copy-done.1
  193.1 0.8 copy-done.5
  193.9 63.4 %shard_map.146.r_2_ = f32[16,16384]{1,0:T(8,128)S(1)} custom-call(s32[128]{0:T(128)S(1)} %get-tuple-element.27.r_0_, s32[128,1,128]{2,1,0:T(1,128)S(1)} %bitcast.81, s32[128,128]{1,0:T(8,128)S(1)} %bitcast.71, bf16[128,128,32]{2,1,0:T(8,128)(2,1)S(1)} %copy-done.1), custom_call_target="tpu_custom_call" | custom-call | tf_op jit(solution)/shard_map/pallas_call | solution.py:194
  257.4 35.8 %shard_map.150 = bf16[16,16384]{1,0:T(8,128)(2,1)S(1)} custom-call(s32[2,64]{1,0:T(2,128)S(1)} %pad_add_fusion.r_0_, s32[1,16384]{1,0:T(1,128)S(1)} %bitcast.72, f32[16,16384]{1,0:T(8,128)S(1)} %shard_map.146.r_2_, f32[16,1]{1,0:T(8,128)S(1)} %copy.42.r_3_, bf16[16,2,64,256]{3,2,1,0:T(8,128)(2,1)S(1)} %all-to-all-done.3.r_4_, ...), custom_call_target="tpu_custom_call" | custom-call | tf_op jit(solution)/shard_map/pallas_call | solution.py:377
  293.2 0.8 copy.53
  294.0 62.3 %all-to-all-start.4 = ((bf16[16,8,2048]{2,0,1:T(8,128)(2,1)}), bf16[16,8,2048]{2,0,1:T(8,128)(2,1)S(1)}, u32[]{:S(2)}, u32[]{:S(2)}) async-start(bf16[16,8,2048]{2,0,1:T(8,128)(2,1)} %bitcast.63), calls=%async_computation.4 | async-start | bytes 1048576 | tf_op jit(solution)/shard_map/all_to_all | solution.py:501
  356.3 0.1 copy.50
  356.4 14.9 %all-to-all-done.4 = bf16[16,8,2048]{2,0,1:T(8,128)(2,1)S(1)} async-done(((bf16[16,8,2048]{2,0,1:T(8,128)(2,1)}), bf16[16,8,2048]{2,0,1:T(8,128)(2,1)S(1)}, u32[]{:S(2)}, u32[]{:S(2)}) %all-to-all-start.4) | async-done | bytes 524320 | tf_op jit(solution)/shard_map/all_to_all | solution.py:501
  371.3 7.9 %shard_map.151 = f32[256,128]{1,0:T(8,128)S(1)} custom-call(bf16[16,16384]{1,0:T(8,128)(2,1)S(1)} %bitcast.75, f32[1,16384]{1,0:T(1,128)S(1)} %bitcast.80, s32[1,16384]{1,0:T(1,128)S(1)} %bitcast.77), custom_call_target="tpu_custom_call" | custom-call | tf_op jit(solution)/shard_map/pallas_call | solution.py:423
  379.2 0.7 reshape.80
  (28 shorter events, 0.3 us)
Async XLA Ops:
  6.5 169.6 %copy-start = (f32[16,32]{1,0:T(8,128)S(1)}, f32[16,32]{1,0:T(8,128)}, u32[]{:S(2)}) copy-start(f32[16,32]{1,0:T(8,128)} %param.21) | copy-start | bytes 6148
  6.5 10.9 %sort.37.cloned.1.call-start = ((), (), s32[]{:S(2)}) async-start(), calls=%async_computation.6 | async-start | bytes 786464 | tf_op jit(solution)/shard_map/sort | solution.py:462
  20.0 16.0 %all-to-all-start = ((f32[8,2,2048]{2,1,0:T(2,128)}), f32[8,2,2048]{2,1,0:T(2,128)S(1)}, u32[]{:S(2)}, u32[]{:S(2)}) async-start(f32[8,2,2048]{2,1,0:T(2,128)} %pad_maximum_fusion.1), calls=%async_computation | async-start | bytes 262144 | tf_op jit(solution)/shard_map/all_to_all | solution.py:469
  36.0 20.0 %all-to-all-start.1 = ((bf16[16,8,2048]{2,0,1:T(8,128)(2,1)}), bf16[16,8,2048]{2,0,1:T(8,128)(2,1)S(1)}, u32[]{:S(2)}, u32[]{:S(2)}) async-start(bf16[16,8,2048]{2,0,1:T(8,128)(2,1)} %bitcast.64), calls=%async_computation.1 | async-start | bytes 1048576 | tf_op jit(solution)/shard_map/all_to_all | solution.py:472
  56.0 87.1 %copy-start.2 = (bf16[8,2,8,2048]{3,2,0,1:T(8,128)(2,1)}, bf16[8,2,8,2048]{3,2,0,1:T(8,128)(2,1)S(1)}, u32[]{:S(2)}) copy-start(bf16[8,2,8,2048]{3,2,0,1:T(8,128)(2,1)S(1)} %copy.47) | copy-start | bytes 1572868
  56.1 0.8 copy-start.3
  56.8 0.7 copy-start.7
  151.1 13.8 %copy-start.9 = (f32[16]{0:T(128)S(1)}, f32[16]{0:T(128)}, u32[]{:S(2)}) copy-start(f32[16]{0:T(128)} %param.23) | copy-start | bytes 196
  159.0 98.4 %all-to-all-start.3 = ((bf16[16,2,64,256]{3,2,1,0:T(8,128)(2,1)}), bf16[16,2,64,256]{3,2,1,0:T(8,128)(2,1)S(1)}, u32[]{:S(2)}, u32[]{:S(2)}) async-start(bf16[16,2,64,256]{3,2,1,0:T(8,128)(2,1)} %bitcast.20), calls=%async_computation.3 | async-start | bytes 2097152 | tf_op jit(solution)/shard_map/all_to_all | solution.py:497
  164.0 12.2 %all-gather.2.cloned.1.call-start = ((), (), s32[]{:S(2)}) async-start(), calls=%async_computation.5 | async-start | bytes 1572864 | tf_op jit(solution)/shard_map/all_gather | solution.py:475
  164.7 26.2 %sort.39.cloned.1.call-start = ((), (), s32[]{:S(2)}) async-start(), calls=%async_computation.7 | async-start | bytes 196640 | tf_op jit(solution)/shard_map/sort | solution.py:192
  184.9 72.5 %copy-start.4 = (bf16[128,128]{1,0:T(8,128)(2,1)S(1)}, bf16[128,128]{1,0:T(8,128)(2,1)}, u32[]{:S(2)}) copy-start(bf16[128,128]{1,0:T(8,128)(2,1)} %constant.10.clone.r_4_.r_5_) | copy-start | bytes 98308
  184.9 72.5 %copy-start.6 = (bf16[64,128]{1,0:T(8,128)(2,1)S(1)}, bf16[64,128]{1,0:T(8,128)(2,1)}, u32[]{:S(2)}) copy-start(bf16[64,128]{1,0:T(8,128)(2,1)} %constant.27.clone.r_6_) | copy-start | bytes 49156
  184.9 171.4 %copy-start.8 = (f32[8,2048]{1,0:T(8,128)S(1)}, f32[8,2048]{1,0:T(8,128)}, u32[]{:S(2)}) copy-start(f32[8,2048]{1,0:T(8,128)} %get-tuple-element.12) | copy-start | bytes 196612
  190.9 2.2 copy-start.1
  193.1 0.8 copy-start.5
  294.0 77.2 %all-to-all-start.4 = ((bf16[16,8,2048]{2,0,1:T(8,128)(2,1)}), bf16[16,8,2048]{2,0,1:T(8,128)(2,1)S(1)}, u32[]{:S(2)}, u32[]{:S(2)}) async-start(bf16[16,8,2048]{2,0,1:T(8,128)(2,1)} %bitcast.63), calls=%async_computation.4 | async-start | bytes 1048576 | tf_op jit(solution)/shard_map/all_to_all | solution.py:501
Sparse Core Ops, SparseCore 0:
  9.9 7.2 sort.41.cloned.1.call-done
  166.4 9.6 all-gather.1
  178.4 5.6 sort.43.cloned.1.call-done
  (2 shorter events, 0.0 us)
